TPU v7x, 256 devices: a whole 4x4x8 slice. The times are simulated.
256 devices in a mesh: group: 16 (over y, x), ingroup: 16 (over z, core).
Axes of the slice: x: 4, y: 4, z: 8, core: 2. Of those that a mesh axis runs over, the one named last changes fastest.
Arguments:
- activations: bfloat16 [16384, 3584], P(('group', 'ingroup')), may hold values from -6 to 6
- gate_weights: bfloat16 [256, 1792, 1024], P(('group', 'ingroup')), may hold values from -0.09375 to 0.09375
- up_weights: bfloat16 [256, 1792, 1024], P(('group', 'ingroup')), may hold values from -0.09375 to 0.09375
- down_weights: bfloat16 [256, 1024, 1792], P(('group', 'ingroup')), may hold values from -0.375 to 0.375
- expert_ids: int32 [16384, 8], P(('group', 'ingroup')), may hold values from 0 to 127, as said below
- gate_scores: int32 [16384, 8], P(('group', 'ingroup')), may hold values from 1 to 15
- arrival_pos: int32 [16384], P(('group', 'ingroup')), may hold values from 0 to 63, as said below
Outputs:
- expert_mix: bfloat16 [16384, 3584], P(('group', 'ingroup'))
Inputs may be any that keep to these rules, and one draw needn't show every extreme that they name: `expert_ids`: each row names 8 different experts, two from each of 4 different groups. Among one device's 64 rows no expert is named more than 6 times and no group by more than 24 rows; on every device some expert is named exactly 6 times and some group by exactly 24 rows. `arrival_pos`: within each device's 64 rows the values are a permutation.
All inputs are finite; a program needn't handle non-finite values.
Results may differ from a plain program's by a relative error of at most 0.0077.
Values may be sent and summed in bfloat16 or wider, within the bound.
No kernel may reach another device: no remote copies, remote signals or barrier semaphores. Data moves between devices by JAX's collectives and lax.ppermute only.
A program may use at most 128 MiB of HBM per device.

v0:
```python
import jax
import jax.numpy as jnp
from jax import lax
from jax.sharding import PartitionSpec as P

TOPG = 4


def from_partner(shard, axis, apart):
    return lax.ppermute(shard, axis, [(i, i ^ 1 << apart) for i in range(lax.axis_size(axis))])


def group_layout(int_table, groups, members, expert_most):
    shaped = int_table.reshape(groups, members // 2, 1, expert_most)
    shaped = jnp.broadcast_to(shaped, (groups, members // 2, 2, expert_most))
    return shaped.reshape(groups, members, expert_most)


def per_device(
    activations, gate_weights, up_weights, down_weights, expert_ids, gate_scores, arrival_pos
):
    groups = lax.axis_size("group")
    members = lax.axis_size("ingroup")
    per_group = members // 2
    experts = groups * per_group
    tok_count = activations.shape[0]
    model_width = activations.shape[1]
    half_width = model_width // 2
    top_picks = expert_ids.shape[1]
    capacity = 2 * top_picks * tok_count
    group_most = min(tok_count, 3 * tok_count * TOPG // (2 * groups))
    expert_most = (2 * group_most + per_group - 1) // per_group
    expert_range = jnp.arange(experts, dtype=jnp.int32)
    pick_hits = (expert_ids[:, :, None] == expert_range[None, None, :]).astype(jnp.int32)
    hit_table = jnp.sum(pick_hits, axis=1)
    occurrence = jnp.cumsum(hit_table, axis=0) - hit_table
    position_range = jnp.arange(tok_count, dtype=jnp.int32)
    arrival_table = (arrival_pos[:, None] == position_range[None, :]).astype(jnp.int32)
    own_counts = jnp.dot(hit_table.T, arrival_table)
    shifts = jnp.arange(32, dtype=jnp.int32)
    flat_bits = own_counts.reshape(-1, 32)
    packed = jnp.sum(jnp.left_shift(flat_bits, shifts[None, :]), axis=1)[None, :]
    my_index = lax.axis_index(("group", "ingroup"))
    piece = lax.all_gather(packed, ("group", "ingroup"), axis=0, tiled=True)
    bit_table = jnp.bitwise_and(jnp.right_shift(piece[:, :, None], shifts[None, None, :]), 1)
    bit_table = bit_table.reshape(piece.shape[0], experts, tok_count)
    source_index = jnp.arange(piece.shape[0], dtype=jnp.int32)
    earlier_flag = (source_index < my_index).astype(jnp.int32)
    prior_part = jnp.sum(bit_table * earlier_flag[:, None, None], axis=0)
    total_part = jnp.sum(bit_table, axis=0)
    earlier = jnp.cumsum(total_part, axis=1) - total_part
    rank_table = earlier + prior_part
    rank_by_token = jnp.dot(arrival_table, rank_table.T)
    pick_rank = jnp.sum(pick_hits * rank_by_token[:, None, :], axis=2)
    pick_occurrence = jnp.sum(pick_hits * occurrence[:, None, :], axis=2)
    kept_mask = (pick_rank < capacity).astype(jnp.int32)
    kept_scores = gate_scores * kept_mask
    weight_sum = jnp.maximum(jnp.sum(kept_scores, axis=1), 1)
    routing = kept_scores.astype(jnp.float32) / weight_sum.astype(jnp.float32)[:, None]
    slot_range = jnp.arange(expert_most, dtype=jnp.int32)
    slot_match = hit_table[:, :, None] * (
        occurrence[:, :, None] == slot_range[None, None, :]
    ).astype(jnp.int32)
    slot_valid = jnp.sum(slot_match, axis=0)
    slot_token = jnp.sum(slot_match * position_range[:, None, None], axis=0)
    slot_rank = jnp.sum(slot_match * rank_by_token[:, :, None], axis=0)
    send_rank = jnp.where((slot_valid > 0) & (slot_rank < capacity), slot_rank, -1)
    half_index = jnp.arange(members, dtype=jnp.int32) % 2
    token_layout = jnp.transpose(group_layout(slot_token, groups, members, expert_most), (1, 0, 2))
    rank_layout = jnp.transpose(group_layout(send_rank, groups, members, expert_most), (1, 0, 2))
    feature_rows = activations.reshape(tok_count * 2, half_width)
    send_rows = jnp.take(feature_rows, token_layout * 2 + half_index[:, None, None], axis=0)
    got_rows, got_rank = (
        lax.all_to_all(
            lax.all_to_all(send_rows, "group", split_axis=1, concat_axis=1, tiled=True),
            "ingroup",
            split_axis=0,
            concat_axis=0,
            tiled=True,
        ),
        lax.all_to_all(
            lax.all_to_all(rank_layout, "group", split_axis=1, concat_axis=1, tiled=True),
            "ingroup",
            split_axis=0,
            concat_axis=0,
            tiled=True,
        ),
    )
    slot_total = members * groups * expert_most
    flat_rank = got_rank.reshape(slot_total)
    flat_rows = got_rows.reshape(slot_total, half_width)
    target = jnp.where(flat_rank >= 0, flat_rank, capacity)
    source_of = (
        jnp.zeros((capacity,), jnp.int32)
        .at[target]
        .set(jnp.arange(slot_total, dtype=jnp.int32), mode="drop")
    )
    filled = jnp.zeros((capacity,), jnp.bool_).at[target].set(True, mode="drop")
    expert_rows = jnp.where(
        filled[:, None], jnp.take(flat_rows, source_of, axis=0), jnp.zeros((), activations.dtype)
    )
    gate_part = jnp.dot(expert_rows, gate_weights[0], preferred_element_type=jnp.float32).astype(
        jnp.bfloat16
    )
    up_part = jnp.dot(expert_rows, up_weights[0], preferred_element_type=jnp.float32).astype(
        jnp.bfloat16
    )
    other_gate, other_up = from_partner((gate_part, up_part), "ingroup", 0)
    gate_sum = gate_part.astype(jnp.float32) + other_gate.astype(jnp.float32)
    up_sum = up_part.astype(jnp.float32) + other_up.astype(jnp.float32)
    hidden = (jax.nn.silu(gate_sum) * up_sum).astype(jnp.bfloat16)
    expert_out = jnp.dot(hidden, down_weights[0], preferred_element_type=jnp.float32).astype(
        jnp.bfloat16
    )
    back_rows = jnp.take(expert_out, jnp.clip(flat_rank, 0, capacity - 1), axis=0)
    back_rows = jnp.where((flat_rank >= 0)[:, None], back_rows, jnp.zeros((), jnp.bfloat16))
    back_rows = back_rows.reshape(members, groups, expert_most, half_width)
    pick_group = expert_ids // per_group
    returned = lax.all_to_all(
        lax.all_to_all(back_rows, "group", split_axis=1, concat_axis=1, tiled=True),
        "ingroup",
        split_axis=0,
        concat_axis=0,
        tiled=True,
    )
    pick_member = expert_ids % per_group * 2
    halves = jnp.arange(2, dtype=jnp.int32)
    flat_pick = (
        (pick_member[:, :, None] + halves[None, None, :]) * groups + pick_group[:, :, None]
    ) * expert_most + pick_occurrence[:, :, None]
    gathered = jnp.take(returned.reshape(slot_total, half_width), flat_pick, axis=0)
    terms = routing[:, :, None] * gathered.reshape(tok_count, top_picks, model_width).astype(
        jnp.float32
    )
    pick_range = jnp.arange(top_picks, dtype=jnp.int32)
    not_self = (pick_range[:, None] != pick_range[None, :]).astype(jnp.int32)
    same_other = (pick_group[:, :, None] == pick_group[:, None, :]).astype(jnp.int32) * not_self[
        None, :, :
    ]
    partner = jnp.sum(same_other * pick_range[None, None, :], axis=2)
    partner_terms = jnp.take_along_axis(terms, partner[:, :, None], axis=1)
    paired = terms + partner_terms
    rounded = lax.optimization_barrier(paired.astype(jnp.bfloat16)).astype(jnp.float32)
    combined = 0.5 * jnp.sum(rounded, axis=1)
    return combined.astype(jnp.bfloat16)


def solution(mesh):
    return jax.shard_map(
        per_device,
        mesh=mesh,
        in_specs=(
            P(("group", "ingroup"), None),
            P(("group", "ingroup"), None, None),
            P(("group", "ingroup"), None, None),
            P(("group", "ingroup"), None, None),
            P(("group", "ingroup"), None),
            P(("group", "ingroup"), None),
            P(("group", "ingroup")),
        ),
        out_specs=P(("group", "ingroup"), None),
        check_vma=False,
    )
```

profile of v0, /device:TPU:8, one launch (start us, length us, event | category | flops | bytes accessed | tf_op | source)
XLA Modules:
  0.0 713.9 jit_solution(8007721992500397717)
XLA Ops:
  0.0 0.8 copy.125
  1.0 0.9 fusion.22
  2.1 65.1 %all-gather.1 = s32[256,1,256]{2,1,0:T(1,128)S(1)} all-gather(s32[1,1,256]{2,1,0:T(1,128)S(1)} %bitcast.53), channel_id=2, replica_groups=mesh['group'=16,'ingroup'=16] {'group','ingroup'}, dimensions={0}, use_global_device_ids=true | all-gather | bytes 263168 | tf_op jit(solution)/shard_map/all_gather | solution.py:44
  67.3 1.7 fusion
  69.8 0.9 fusion.19
  71.0 0.7 copy.142
  71.7 5.4 all-to-all-start
  78.1 6.7 gather_fusion
  84.8 9.6 %reshape.253 = bf16[16,16,6,1792]{3,2,1,0:T(8,128)(2,1)} reshape(bf16[1536,1792]{1,0:T(8,128)(2,1)} %gather_fusion) | data formatting | bytes 11010048 | tf_op jit(solution)/shard_map/jit(_take)/gather | solution.py:72
  94.6 4.0 broadcast_select_fusion
  98.6 5.5 copy.150
  104.1 7.2 %all-to-all-start.2 = ((bf16[16,16,6,1792]{3,0,2,1:T(8,128)(2,1)}), bf16[16,16,6,1792]{3,0,2,1:T(8,128)(2,1)}, u32[]{:S(2)}, u32[]{:S(2)}) async-start(bf16[16,16,6,1792]{3,0,2,1:T(8,128)(2,1)} %copy.150), calls=%async_computation.2 | async-start | bytes 11010048 | tf_op jit(solution)/shard_map/all_to_all | solution.py:75
  111.3 0.7 copy.143
  112.0 80.0 %all-to-all-done.2 = bf16[16,16,6,1792]{3,0,2,1:T(8,128)(2,1)} async-done(((bf16[16,16,6,1792]{3,0,2,1:T(8,128)(2,1)}), bf16[16,16,6,1792]{3,0,2,1:T(8,128)(2,1)}, u32[]{:S(2)}, u32[]{:S(2)}) %all-to-all-start.2) | async-done | bytes 5505056 | tf_op jit(solution)/shard_map/all_to_all | solution.py:75
  192.0 4.4 all-to-all-start.1
  196.4 7.9 %copy.151 = bf16[16,16,6,1792]{3,1,2,0:T(8,128)(2,1)} copy(bf16[16,16,6,1792]{3,0,2,1:T(8,128)(2,1)} %all-to-all-done.2) | data formatting | bytes 11010048 | tf_op jit(solution)/shard_map/all_to_all | solution.py:75
  204.3 7.4 %all-to-all-start.3 = ((bf16[16,16,6,1792]{3,1,2,0:T(8,128)(2,1)}), bf16[16,16,6,1792]{3,1,2,0:T(8,128)(2,1)}, u32[]{:S(2)}, u32[]{:S(2)}) async-start(bf16[16,16,6,1792]{3,1,2,0:T(8,128)(2,1)} %copy.151), calls=%async_computation.3 | async-start | bytes 11010048 | tf_op jit(solution)/shard_map/all_to_all | solution.py:74
  212.0 6.2 scatter_custom_fusion.1
  218.2 11.6 %scatter_custom_fusion = pred[1024]{0:T(1024)(128)(4,1)S(1)} fusion(s32[1536]{0:T(1024)S(1)} %get-tuple-element.13, pred[1536]{0:T(1024)(128)(4,1)S(1)} %broadcast.331, pred[]{:T(512)} %constant.148.clone.1), kind=kCustom, calls=%fused_computation.100 | custom fusion | bytes 1025 | tf_op jit(solution)/shard_map/scatter | solution.py:98
  229.9 104.2 %all-to-all-done.3 = bf16[16,16,6,1792]{3,1,2,0:T(8,128)(2,1)} async-done(((bf16[16,16,6,1792]{3,1,2,0:T(8,128)(2,1)}), bf16[16,16,6,1792]{3,1,2,0:T(8,128)(2,1)}, u32[]{:S(2)}, u32[]{:S(2)}) %all-to-all-start.3) | async-done | bytes 5505056 | tf_op jit(solution)/shard_map/all_to_all | solution.py:74
  334.1 7.7 %copy.152 = bf16[16,16,6,1792]{3,2,1,0:T(8,128)(2,1)} copy(bf16[16,16,6,1792]{3,1,2,0:T(8,128)(2,1)} %all-to-all-done.3) | data formatting | bytes 11010048 | tf_op jit(solution)/shard_map/all_to_all | solution.py:74
  341.8 9.7 %reshape.249 = bf16[1536,1792]{1,0:T(8,128)(2,1)} reshape(bf16[16,16,6,1792]{3,2,1,0:T(8,128)(2,1)} %copy.152) | data formatting | bytes 11010048 | tf_op jit(solution)/shard_map/reshape | solution.py:91
  351.5 11.2 %gather_fusion.1 = bf16[1024,1792]{1,0:T(8,128)(2,1)} fusion(bf16[1536,1792]{1,0:T(8,128)(2,1)} %reshape.249, s32[1024]{0:T(1024)S(1)} %fusion.37), kind=kCustom, calls=%fused_computation.1 | custom fusion | bytes 7344128 | tf_op jit(solution)/shard_map/jit(_take)/gather | solution.py:100
  362.7 7.3 %fusion.10 = bf16[1024,1024]{1,0:T(8,128)(2,1)S(1)} fusion(bf16[1,1792,1024]{2,1,0:T(8,128)(2,1)} %param.8, bf16[1024,1792]{1,0:T(8,128)(2,1)} %gather_fusion.1, pred[1024]{0:T(1024)(128)(4,1)S(1)} %compare_and_fusion.3, pred[1024]{0:T(1024)(128)(4,1)S(1)} %scatter_custom_fusion), kind=kOutput, calls=%fused_computation.28 | convolution fusion | flops 3762814976 | bytes 9439232 | tf_op jit(solution)/shard_map/dot_general | solution.py:102
  370.1 5.6 fusion.13
  375.7 0.6 collective-permute-start.1
  376.8 3.7 collective-permute-done.1
  380.4 10.9 %convolution_convert_fusion = bf16[1024,1792]{1,0:T(8,128)(2,1)} fusion(bf16[1,1024,1792]{2,1,0:T(8,128)(2,1)} %param.10, bf16[1024,1024]{1,0:T(8,128)(2,1)} %collective-permute-done.1, bf16[1024,1024]{1,0:T(8,128)(2,1)} %fusion.13, bf16[1024,1024]{1,0:T(8,128)(2,1)} %collective-permute-done, bf16[1024,1024]{1,0:T(8,128)(2,1)S(1)} %fusion.10), kind=kOutput, calls=%fused_computation.18 | convolution fusion | flops 3772514304 | bytes 15728640 | tf_op jit(solution)/shard_map/dot_general | solution.py:112
  391.4 13.9 %gather_fusion.2 = bf16[1536,1792]{1,0:T(8,128)(2,1)} fusion(bf16[1024,1792]{1,0:T(8,128)(2,1)} %convolution_convert_fusion, s32[2048]{0:T(1024)S(1)} %pad_clamp_fusion), kind=kCustom, calls=%fused_computation.2 | custom fusion | bytes 11016192 | tf_op jit(solution)/shard_map/jit(_take)/gather | solution.py:115
  405.2 9.6 %gather.25 = bf16[16,16,6,1792]{3,2,1,0:T(8,128)(2,1)} reshape(bf16[1536,1792]{1,0:T(8,128)(2,1)} %gather_fusion.2) | data formatting | bytes 11010048 | tf_op jit(solution)/shard_map/jit(_take)/gather | solution.py:115
  414.8 4.4 select_select_fusion
  419.2 3.0 copy.153
  422.2 70.0 %all_to_all.30 = bf16[16,16,6,1792]{3,0,2,1:T(8,128)(2,1)S(1)} all-to-all(bf16[16,16,6,1792]{3,0,2,1:T(8,128)(2,1)S(1)} %copy.153), channel_id=1, replica_groups=mesh['group'=16,'ingroup'=16] {'group'}, dimensions={1} | all-to-all | bytes 11010048 | tf_op jit(solution)/shard_map/all_to_all | solution.py:120
  492.2 5.4 copy.154
  497.6 4.9 all-to-all-start.5
  502.4 2.3 select_reduce_fusion.2
  506.6 118.3 %all-to-all-done.5 = bf16[16,16,6,1792]{3,1,2,0:T(8,128)(2,1)} async-done(((bf16[16,16,6,1792]{3,1,2,0:T(8,128)(2,1)}), bf16[16,16,6,1792]{3,1,2,0:T(8,128)(2,1)}, u32[]{:S(2)}, u32[]{:S(2)}) %all-to-all-start.5) | async-done | bytes 5505056 | tf_op jit(solution)/shard_map/all_to_all | solution.py:119
  624.9 7.7 %copy.155 = bf16[16,16,6,1792]{3,2,1,0:T(8,128)(2,1)} copy(bf16[16,16,6,1792]{3,1,2,0:T(8,128)(2,1)} %all-to-all-done.5) | data formatting | bytes 11010048 | tf_op jit(solution)/shard_map/all_to_all | solution.py:119
  632.6 9.7 %reshape.250 = bf16[1536,1792]{1,0:T(8,128)(2,1)} reshape(bf16[16,16,6,1792]{3,2,1,0:T(8,128)(2,1)} %copy.155) | data formatting | bytes 11010048 | tf_op jit(solution)/shard_map/reshape | solution.py:131
  642.3 11.2 %gather_fusion.3 = bf16[1024,1792]{1,0:T(8,128)(2,1)} fusion(bf16[1536,1792]{1,0:T(8,128)(2,1)} %reshape.250, s32[1024]{0:T(1024)S(1)} %broadcast_clamp_fusion), kind=kCustom, calls=%fused_computation.3 | custom fusion | bytes 7344128 | tf_op jit(solution)/shard_map/jit(_take)/gather | solution.py:131
  653.4 8.6 %reshape.277 = bf16[64,8,2,1792]{3,2,1,0:T(2,128)(2,1)} reshape(bf16[1024,1792]{1,0:T(8,128)(2,1)} %gather_fusion.3) | data formatting | bytes 7340032 | tf_op jit(solution)/shard_map/jit(_take)/gather | solution.py:131
  662.0 8.5 %fusion.3 = f32[64,8,2,1792]{3,2,1,0:T(2,128)} fusion(bf16[64,8,2,1792]{3,2,1,0:T(2,128)(2,1)} %reshape.277, pred[64,8,2]{2,1,0:T(8,128)(4,1)S(1)} %copy.140), kind=kLoop, calls=%fused_computation.19 | loop fusion | flops 3670016 | bytes 11011072 | tf_op jit(solution)/shard_map/convert_element_type | solution.py:132
  670.6 10.0 %reshape.251 = f32[64,8,3584]{2,1,0:T(8,128)} reshape(f32[64,8,2,1792]{3,2,1,0:T(2,128)} %fusion.3) | data formatting | bytes 14680064 | tf_op jit(solution)/shard_map/convert_element_type | solution.py:132
  680.6 6.9 broadcast_multiply_fusion
  687.4 16.6 %gather_fusion.4 = f32[512,3584]{1,0:T(8,128)} fusion(f32[64,8,3584]{2,1,0:T(8,128)} %broadcast_multiply_fusion, s32[512]{0:T(512)S(1)} %reshape.284), kind=kCustom, calls=%fused_computation.4 | custom fusion | bytes 14684160 | tf_op jit(solution)/shard_map/jit(take_along_axis)/gather | solution.py:141
  704.0 6.2 fusion.2
  710.2 2.4 convert_reduce_fusion
  712.7 0.8 multiply_convert_fusion.2
  (79 shorter events, 5.2 us)
Async XLA Ops:
  0.0 77.9 %copy-start.1 = (bf16[64,3584]{1,0:T(8,128)(2,1)S(1)}, bf16[64,3584]{1,0:T(8,128)(2,1)}, u32[]{:S(2)}) copy-start(bf16[64,3584]{1,0:T(8,128)(2,1)} %param.7) | copy-start | bytes 1376260
  71.7 32.3 %all-to-all-start = ((s32[16,16,6]{0,2,1:T(8,128)}), s32[16,16,6]{0,2,1:T(8,128)S(1)}, u32[]{:S(2)}, u32[]{:S(2)}) async-start(s32[16,16,6]{0,2,1:T(8,128)} %copy.142), calls=%async_computation | async-start | bytes 131072 | tf_op jit(solution)/shard_map/all_to_all | solution.py:82
  104.1 87.9 %all-to-all-start.2 = ((bf16[16,16,6,1792]{3,0,2,1:T(8,128)(2,1)}), bf16[16,16,6,1792]{3,0,2,1:T(8,128)(2,1)}, u32[]{:S(2)}, u32[]{:S(2)}) async-start(bf16[16,16,6,1792]{3,0,2,1:T(8,128)(2,1)} %copy.150), calls=%async_computation.2 | async-start | bytes 11010048 | tf_op jit(solution)/shard_map/all_to_all | solution.py:75
  192.0 12.3 %all-to-all-start.1 = ((s32[16,16,6]{1,2,0:T(8,128)}), s32[16,16,6]{1,2,0:T(8,128)S(1)}, u32[]{:S(2)}, u32[]{:S(2)}) async-start(s32[16,16,6]{1,2,0:T(8,128)} %copy.143), calls=%async_computation.1 | async-start | bytes 131072 | tf_op jit(solution)/shard_map/all_to_all | solution.py:81
  204.3 129.8 %all-to-all-start.3 = ((bf16[16,16,6,1792]{3,1,2,0:T(8,128)(2,1)}), bf16[16,16,6,1792]{3,1,2,0:T(8,128)(2,1)}, u32[]{:S(2)}, u32[]{:S(2)}) async-start(bf16[16,16,6,1792]{3,1,2,0:T(8,128)(2,1)} %copy.151), calls=%async_computation.3 | async-start | bytes 11010048 | tf_op jit(solution)/shard_map/all_to_all | solution.py:74
  362.7 7.4 %copy-start = (bf16[1024,1792]{1,0:T(8,128)(2,1)S(1)}, bf16[1024,1792]{1,0:T(8,128)(2,1)}, u32[]{:S(2)}) copy-start(bf16[1024,1792]{1,0:T(8,128)(2,1)} %gather_fusion.1) | copy-start | bytes 11010052
  362.7 7.4 %copy-start.3 = (bf16[1,1792,1024]{2,1,0:T(8,128)(2,1)S(1)}, bf16[1,1792,1024]{2,1,0:T(8,128)(2,1)}, u32[]{:S(2)}) copy-start(bf16[1,1792,1024]{2,1,0:T(8,128)(2,1)} %param.9) | copy-start | bytes 11010052
  370.0 6.8 collective-permute-start
  375.7 4.7 collective-permute-start.1
  497.6 8.1 %copy-start.2 = (s32[64,8]{0,1:T(8,128)S(1)}, s32[64,8]{0,1:T(8,128)}, u32[]{:S(2)}) copy-start(s32[64,8]{0,1:T(8,128)} %param.12) | copy-start | bytes 6148
  497.6 127.3 %all-to-all-start.5 = ((bf16[16,16,6,1792]{3,1,2,0:T(8,128)(2,1)}), bf16[16,16,6,1792]{3,1,2,0:T(8,128)(2,1)}, u32[]{:S(2)}, u32[]{:S(2)}) async-start(bf16[16,16,6,1792]{3,1,2,0:T(8,128)(2,1)} %copy.154), calls=%async_computation.5 | async-start | bytes 11010048 | tf_op jit(solution)/shard_map/all_to_all | solution.py:119
where the time goes:
time: 726 us; the launch traced here: 714 us
  waiting for transfers between devices  306 us (42%)
  local copies, waits for them, and re-layouts  177 us (24%)
  blocking collectives  135 us (19%)
  other arithmetic  38.8 us (5%)
  starting transfers between devices  29.9 us (4%)
  matrix products  25.6 us (4%)
    all_to_all x1, waiting for transfers between devices, per_device(): lax.all_to_all(lax.all_to_all(back_rows, 'group', split_axis=1, concat_ax...  118 us
    all_to_all x1, waiting for transfers between devices, per_device(): lax.all_to_all(lax.all_to_all(send_rows, 'group', split_axis=1, concat_ax...  104 us
    all_to_all x1, waiting for transfers between devices, per_device(): lax.all_to_all(send_rows, 'group', split_axis=1, concat_axis=1, tiled=True)  80 us
    all_to_all x1, blocking collectives, per_device(): lax.all_to_all(back_rows, 'group', split_axis=1, concat_axis=1, tiled=True)  70 us
    all_gather x1, blocking collectives, per_device(): piece = lax.all_gather(packed, ('group', 'ingroup'), axis=0, tiled=True)  65.1 us
    gather x2, local copies, waits for them, and re-layouts, per_device(): jnp.take(expert_out, jnp.clip(flat_rank, 0, capacity - 1), axis=0)  23.4 us
    gather x2, local copies, waits for them, and re-layouts, per_device(): jnp.take(returned.reshape(slot_total, half_width), flat_pick, axis=0)  19.8 us
    gather x3, local copies, waits for them, and re-layouts, per_device(): partner_terms = jnp.take_along_axis(terms, partner[:, :, None], axis=1)  16.8 us
  transfers between devices with their start and end apart: 7, of which 4 were waited for; matrix products, arithmetic and copies ran while one was open for 9% of the time, Pallas kernels for 0%

commit v1 on v0

v1 whole, which is shorter than its diff:
```python
import functools

import jax
import jax.numpy as jnp
from jax import lax
from jax.experimental import pallas as pl
from jax.experimental.pallas import tpu as pltpu
from jax.sharding import PartitionSpec as P

TOPG = 4
META = 128
AT_SCORE, AT_POS, AT_ONE = 8, 16, 17
EMPTY = 1.0e9
NEAR = (0, -1, 1, -2)
FAR = (2, -3, 3, -4)
F32, BF16 = jnp.float32, jnp.bfloat16


def iota(shape, axis):
    return lax.broadcasted_iota(jnp.int32, shape, axis)


def divided(value, by, most):
    total = jnp.zeros_like(value)
    for j in range(1, most):
        total = total + (value >= j * by).astype(jnp.int32)
    return total


def tiles(width, tile):
    return [(at, min(tile, width - at)) for at in range(0, width, tile)]


def call(kernel, name, out_shape, flops, moved, vmem, **more):
    return pl.pallas_call(
        kernel,
        out_shape=out_shape,
        name=name,
        cost_estimate=pl.CostEstimate(flops=flops, bytes_accessed=moved, transcendentals=0),
        compiler_params=pltpu.CompilerParams(vmem_limit_bytes=vmem << 20),
        **more,
    )


def pick_rows_kernel(place_ref, *refs, groups, per_group, slots):
    blocks, out_ref = refs[:-1], refs[-1]
    tok, width = blocks[0].shape
    feat = width - META
    total = tok * len(blocks)
    rows = slots * len(blocks)
    meta = jnp.concatenate([b[:, feat:] for b in blocks], axis=0)
    unit = (iota((32, META), 0) == iota((32, META), 1)).astype(F32).astype(BF16)
    meta_t = lax.dot_general(unit, meta, (((1,), (1,)), ((), ())), preferred_element_type=F32)
    expert = (iota((groups, total), 0) * per_group + place_ref[0]).astype(F32)
    hit = jnp.zeros((groups, total), F32)
    for k in range(AT_SCORE):
        hit = hit + (meta_t[k : k + 1, :] == expert).astype(F32)
    first, second = iota((total, total), 0), iota((total, total), 1)
    same = divided(first, tok, len(blocks)) == divided(second, tok, len(blocks))
    before = (same & (first < second)).astype(F32).astype(BF16)
    occurrence = jnp.dot(hit.astype(BF16), before, preferred_element_type=F32)
    block_of = divided(iota((groups, total), 1), tok, len(blocks)).astype(F32)
    slot = jnp.where(hit > 0, occurrence + slots * block_of, -1.0)
    slot = jnp.broadcast_to(slot[:, None, :], (groups, rows, total))
    chosen = (slot == iota((groups, rows, total), 1).astype(F32)).astype(F32)
    chosen = chosen.reshape(groups * rows, total).astype(BF16)
    for at, wide in tiles(width, 512):
        part = jnp.concatenate([b[:, at : at + wide] for b in blocks], axis=0)
        out_ref[:, at : at + wide] = jnp.dot(chosen, part, preferred_element_type=F32).astype(BF16)


def pick_rows(place, blocks, groups, per_group, slots):
    width = blocks[0].shape[1]
    total = blocks[0].shape[0] * len(blocks)
    rows = groups * slots * len(blocks)
    return call(
        functools.partial(pick_rows_kernel, groups=groups, per_group=per_group, slots=slots),
        "pick_rows",
        jax.ShapeDtypeStruct((rows, width), BF16),
        2 * rows * total * width,
        2 * (rows + total) * width,
        40,
        in_specs=[pl.BlockSpec(memory_space=pltpu.SMEM)]
        + [pl.BlockSpec(memory_space=pltpu.VMEM)] * len(blocks),
        out_specs=pl.BlockSpec(memory_space=pltpu.VMEM),
    )(place, *blocks)


def score_table_kernel(place_ref, *refs, groups, per_group, slots):
    blocks, out_ref = refs[:-1], refs[-1]
    tok = blocks[0].shape[0]
    total = tok * len(blocks)
    rows = slots * len(blocks)
    meta = jnp.concatenate([b[...] for b in blocks], axis=0).astype(F32)
    expert = (iota((total, META), 1) * per_group + place_ref[0]).astype(F32)
    hit = jnp.zeros((total, META), F32)
    score = jnp.zeros((total, META), F32)
    for k in range(AT_SCORE):
        same = (meta[:, k : k + 1] == expert).astype(F32)
        hit = hit + same
        score = score + same * meta[:, AT_SCORE + k : AT_SCORE + k + 1]
    first, second = iota((total, total), 0), iota((total, total), 1)
    same = divided(first, tok, len(blocks)) == divided(second, tok, len(blocks))
    before = (same & (second < first)).astype(F32).astype(BF16)
    occurrence = jnp.dot(before, hit.astype(BF16), preferred_element_type=F32)
    block_of = divided(iota((total, META), 0), tok, len(blocks)).astype(F32)
    slot = jnp.where(hit > 0, occurrence + slots * block_of, -1.0)
    source, lane = iota((META, groups * rows), 0), iota((META, groups * rows), 1)
    spread = ((lane >= source * rows) & (lane < source * rows + rows)).astype(F32).astype(BF16)
    slot_wide = jnp.dot(slot.astype(BF16), spread, preferred_element_type=F32)
    score_wide = jnp.dot(score.astype(BF16), spread, preferred_element_type=F32)
    column = iota((1, groups * rows), 1)
    column = (column - rows * divided(column, rows, groups)).astype(F32)
    out_ref[...] = jnp.where(slot_wide == column, score_wide, 0.0).astype(BF16)


def score_table(place, blocks, groups, per_group, slots):
    tok, width = blocks[0].shape
    total = tok * len(blocks)
    columns = groups * slots * len(blocks)
    last = width // META - 1
    return call(
        functools.partial(score_table_kernel, groups=groups, per_group=per_group, slots=slots),
        "score_table",
        jax.ShapeDtypeStruct((total, columns), BF16),
        2 * total * columns * (2 * META),
        2 * total * columns,
        40,
        grid=(1,),
        in_specs=[pl.BlockSpec(memory_space=pltpu.SMEM)]
        + [pl.BlockSpec((tok, META), lambda i: (0, last))] * len(blocks),
        out_specs=pl.BlockSpec((total, columns), lambda i: (0, 0)),
    )(place, *blocks)


def hidden_kernel(
    place_ref, rows_ref, gate_own, gate_other, up_own, up_other, out_ref, line_ref, column_ref,
    *, groups, members, slots, offsets
):
    count = rows_ref.shape[0]
    half = gate_own.shape[1]
    z, c = place_ref[0], place_ref[1]

    @pl.when(pl.program_id(0) == 0)
    def _():
        meta = rows_ref[:, 2 * half :]
        unit = (iota((32, META), 0) == iota((32, META), 1)).astype(F32).astype(BF16)
        meta_t = lax.dot_general(unit, meta, (((1,), (1,)), ((), ())), preferred_element_type=F32)

        def key(index, position, valid):
            group = divided(index, count // groups, groups)
            block = divided(index - (count // groups) * group, slots, len(offsets))
            apart = jnp.zeros_like(index)
            for j, offset in enumerate(offsets):
                apart = apart + jnp.where(block == j, offset, 0)
            ring = members // 2
            where = z + apart
            where = jnp.where(where < 0, where + ring, where)
            where = jnp.where(where >= ring, where - ring, where)
            source = (group * members + where * 2 + c).astype(F32)
            return jnp.where(valid > 0, position * (groups * members) + source, EMPTY)

        line = key(iota((1, count), 1), meta_t[AT_POS : AT_POS + 1], meta_t[AT_ONE : AT_ONE + 1])
        line_ref[...] = jnp.broadcast_to(line, line_ref.shape)
        wide = meta.astype(F32)
        column = key(
            iota((count, 1), 0), wide[:, AT_POS : AT_POS + 1], wide[:, AT_ONE : AT_ONE + 1]
        )
        column_ref[...] = jnp.broadcast_to(column, column_ref.shape)

    own = rows_ref[:, pl.ds(pl.multiple_of(c * half, 128), half)]
    other = rows_ref[:, pl.ds(pl.multiple_of((1 - c) * half, 128), half)]
    gate = jnp.dot(own, gate_own[0], preferred_element_type=F32) + jnp.dot(
        other, gate_other[0], preferred_element_type=F32
    )
    up = jnp.dot(own, up_own[0], preferred_element_type=F32) + jnp.dot(
        other, up_other[0], preferred_element_type=F32
    )
    out_ref[...] = (gate / (1.0 + jnp.exp(-gate)) * up).astype(BF16)


def hidden_rows(place, rows, gate_own, gate_other, up_own, up_other, groups, members, slots, offsets):
    count, width = rows.shape
    half, units = gate_own.shape[1:]
    tile = 256
    weight = pl.BlockSpec((1, half, tile), lambda i: (0, 0, i))
    return call(
        functools.partial(
            hidden_kernel, groups=groups, members=members, slots=slots, offsets=offsets
        ),
        "hidden_rows",
        (
            jax.ShapeDtypeStruct((count, units), BF16),
            jax.ShapeDtypeStruct((8, count), F32),
            jax.ShapeDtypeStruct((count, META), F32),
        ),
        8 * count * half * units,
        2 * (count * width + 4 * half * units + count * units),
        40,
        grid=(units // tile,),
        in_specs=[
            pl.BlockSpec(memory_space=pltpu.SMEM),
            pl.BlockSpec((count, width), lambda i: (0, 0)),
            weight,
            weight,
            weight,
            weight,
        ],
        out_specs=(
            pl.BlockSpec((count, tile), lambda i: (0, i)),
            pl.BlockSpec((8, count), lambda i: (0, 0)),
            pl.BlockSpec((count, META), lambda i: (0, 0)),
        ),
    )(place, rows, gate_own, gate_other, up_own, up_other)


def down_tiles(hidden_ref, weight_ref, out_ref, tile):
    def step(i, carry):
        columns = pl.ds(pl.multiple_of(i * tile, 128), tile)
        out_ref[:, columns] = jnp.dot(
            hidden_ref[...], weight_ref[0, :, columns], preferred_element_type=F32
        ).astype(BF16)
        return carry

    lax.fori_loop(0, weight_ref.shape[2] // tile, step, 0)


def down_first_kernel(*refs, parts, groups, capacity):
    lines, columns, hiddens = refs[: 2 * parts], refs[2 * parts : 3 * parts], refs[3 * parts : 4 * parts]
    weight_ref, out_ref, all_ref, flag_ref = refs[4 * parts :]
    masked, flags = [], []
    for column_ref, hidden_ref in zip(columns, hiddens):
        own = column_ref[:, :1]
        rank = jnp.zeros(own.shape, F32)
        for line_ref in lines:
            rank = rank + jnp.sum((line_ref[:1, :] < own).astype(F32), axis=1, keepdims=True)
        kept = jnp.where((rank < capacity) & (own < EMPTY), 1.0, 0.0)
        masked.append(hidden_ref[...].astype(F32) * kept)
        flags.append(jnp.broadcast_to(kept, (kept.shape[0], META)))
    part = masked[0].shape[0] // groups
    rows = part * parts
    for g in range(groups):
        cut = slice(g * part, (g + 1) * part)
        to = slice(g * rows, (g + 1) * rows)
        all_ref[to, :] = jnp.concatenate([m[cut] for m in masked], axis=0).astype(BF16)
        flag_ref[to, :] = jnp.concatenate([f[cut] for f in flags], axis=0).astype(BF16)
    down_tiles(all_ref, weight_ref, out_ref, 256)


def down_first(lines, columns, hiddens, weight, groups, capacity):
    count = sum(h.shape[0] for h in hiddens)
    units, half = weight.shape[1:]
    return call(
        functools.partial(
            down_first_kernel, parts=len(hiddens), groups=groups, capacity=capacity
        ),
        "down_first",
        (
            jax.ShapeDtypeStruct((count, half), BF16),
            jax.ShapeDtypeStruct((count, units), BF16),
            jax.ShapeDtypeStruct((count, META), BF16),
        ),
        2 * count * half * units,
        2 * (count * (half + units) + half * units),
        48,
        in_specs=[pl.BlockSpec(memory_space=pltpu.VMEM)] * (4 * len(hiddens) + 1),
        out_specs=(pl.BlockSpec(memory_space=pltpu.VMEM),) * 3,
    )(*lines, *columns, *hiddens, weight)


def down_second_kernel(hidden_ref, flag_ref, weight_ref, out_ref):
    half = weight_ref.shape[2]
    down_tiles(hidden_ref, weight_ref, out_ref, 256)
    out_ref[:, half:] = flag_ref[...]


def down_second(hidden, flags, weight):
    count = hidden.shape[0]
    units, half = weight.shape[1:]
    return call(
        down_second_kernel,
        "down_second",
        jax.ShapeDtypeStruct((count, half + META), BF16),
        2 * count * half * units,
        2 * (count * (half + units) + half * units),
        40,
        in_specs=[pl.BlockSpec(memory_space=pltpu.VMEM)] * 3,
        out_specs=pl.BlockSpec(memory_space=pltpu.VMEM),
    )(hidden, flags, weight)


def combine_kernel(table_ref, rows_ref, *out_refs):
    tok = out_refs[0].shape[0]
    for at, wide in tiles(rows_ref.shape[1], 512):
        part = jnp.dot(table_ref[...], rows_ref[:, at : at + wide], preferred_element_type=F32)
        for b, out_ref in enumerate(out_refs):
            out_ref[:, at : at + wide] = part[b * tok : (b + 1) * tok].astype(BF16)


def combine(table, rows, blocks):
    total, count = table.shape
    width = rows.shape[1]
    return call(
        combine_kernel,
        "combine",
        (jax.ShapeDtypeStruct((total // blocks, width), BF16),) * blocks,
        2 * total * count * width,
        2 * (total * count + (count + total) * width),
        40,
        in_specs=[pl.BlockSpec(memory_space=pltpu.VMEM)] * 2,
        out_specs=(pl.BlockSpec(memory_space=pltpu.VMEM),) * blocks,
    )(table, rows)


def per_device(
    activations, gate_weights, up_weights, down_weights, expert_ids, gate_scores, arrival_pos
):
    groups = lax.axis_size("group")
    members = lax.axis_size("ingroup")
    per_group = ring = members // 2
    tok = activations.shape[0]
    model = activations.shape[1]
    half = model // 2
    top_picks = expert_ids.shape[1]
    capacity = 2 * top_picks * tok
    group_most = min(tok, 3 * tok * TOPG // (2 * groups))
    slots = (2 * group_most + per_group - 1) // per_group
    index = lax.axis_index("ingroup")
    place = jnp.stack([index // 2, index % 2]).astype(jnp.int32)
    partner = [(i, i ^ 1) for i in range(members)]

    def along(shard, by):
        hop = [(i, (i // 2 + by) % ring * 2 + i % 2) for i in range(members)]
        return lax.ppermute(shard, "ingroup", hop)

    def swap(shard):
        return lax.ppermute(shard, "ingroup", partner)

    def exchange(rows):
        return lax.all_to_all(rows, "group", split_axis=0, concat_axis=0, tiled=True)

    extra = jnp.concatenate(
        [
            expert_ids,
            gate_scores,
            arrival_pos[:, None],
            jnp.ones((tok, 1), jnp.int32),
            jnp.zeros((tok, META - 2 * top_picks - 2), jnp.int32),
        ],
        axis=1,
    )
    held = {0: jnp.concatenate([activations, extra.astype(BF16)], axis=1)}
    for step in range(1, ring // 2 + 1):
        held[-step] = along(held[1 - step], 1)
        if step < ring // 2:
            held[step] = along(held[step - 1], -1)
    gate_other, up_other, down_other = swap(gate_weights), swap(up_weights), swap(down_weights)

    lines, columns, hiddens = [], [], []
    for offsets in (NEAR, FAR):
        rows = exchange(
            pick_rows(place, [held[o] for o in offsets], groups, per_group, slots)
        )
        hidden, line, column = hidden_rows(
            place, rows, gate_weights, gate_other, up_weights, up_other,
            groups, members, slots, offsets,
        )
        lines.append(line)
        columns.append(column)
        hiddens.append(hidden)
    order = NEAR + FAR
    table = score_table(place, [held[o] for o in order], groups, per_group, slots)
    lines = lines + [swap(line) for line in lines]
    own_out, hidden, flags = down_first(lines, columns, hiddens, down_weights, groups, capacity)
    other_out = down_second(hidden, flags, down_other)

    halves = []
    for out in (own_out, other_out):
        parts = dict(zip(order, combine(table, exchange(out), len(order))))
        sums = [parts[0].astype(F32)]
        for way in (-1, 1):
            most = ring // 2 if way == -1 else ring // 2 - 1
            moving = parts[way * most]
            for step in range(most - 1, 0, -1):
                moving = along(moving, way)
                moving = (moving.astype(F32) + parts[way * step].astype(F32)).astype(BF16)
            sums.append(along(moving, way).astype(F32))
        halves.append(sum(sums))
    weight_sum = jnp.maximum(halves[1][:, half : half + 1], 1.0)
    own, other = halves[0] / weight_sum, halves[1][:, :half] / weight_sum
    is_first = index % 2 == 0
    left = jnp.where(is_first, own, other)
    right = jnp.where(is_first, other, own)
    return jnp.concatenate([left, right], axis=1).astype(BF16)


def solution(mesh):
    rows = P(("group", "ingroup"), None)
    weights = P(("group", "ingroup"), None, None)
    return jax.shard_map(
        per_device,
        mesh=mesh,
        in_specs=(rows, weights, weights, weights, rows, rows, P(("group", "ingroup"))),
        out_specs=rows,
        check_vma=False,
    )
```

time: 726 us -> 289 us (0.40); the launches traced: 714 us -> 287 us
  waiting for transfers between devices: 306 us -> 146 us
  local copies, waits for them, and re-layouts: 177 us -> 27.7 us
  blocking collectives: 135 us -> 0 us
  Pallas kernels: 0 us -> 46.7 us
  other arithmetic: 38.8 us -> 5.72 us
  starting transfers between devices: 29.9 us -> 60 us
  matrix products: 25.6 us -> 0 us
    all_to_all x5 -> x4, waiting for transfers between devices: 303 us -> 83.8 us  [exchange(): lax.all_to_all(rows, 'group', split_axis=0, concat_axis=0, tiled=True)]
    gather x10 -> x0, local copies, waits for them, and re-layouts: 87.5 us -> none  [the longest x2 23.4 us: per_device(): jnp.take(expert_out, jnp.clip(flat_rank, 0, capacity - 1), axis=0)]
    all_to_all x1 -> x0, blocking collectives: 70 us -> none  [per_device(): lax.all_to_all(back_rows, 'group', split_axis=1, concat_axis=1, tiled=True)]
    all_gather x1 -> x0, blocking collectives: 65.1 us -> none  [per_device(): piece = lax.all_gather(packed, ('group', 'ingroup'), axis=0, tiled=True)]
    ppermute x2 -> x26, waiting for transfers between devices: 3.66 us -> 62.7 us  [the longest x21 61.5 us: along(): return lax.ppermute(shard, 'ingroup', hop)]
    pallas_call x0 -> x9, Pallas kernels: none -> 46.7 us  [the longest x2 19.3 us: hidden_rows(): call(functools.partial(hidden_kernel, groups=groups, members=members, slo...]
    ppermute x2 -> x26, starting transfers between devices: 0.7 us -> 36.2 us  [the longest x21 35.2 us: along(): return lax.ppermute(shard, 'ingroup', hop)]
    all_to_all x6 -> x0, local copies, waits for them, and re-layouts: 29.6 us -> none  [the longest x1 7.91 us: per_device(): lax.all_to_all(send_rows, 'group', split_axis=1, concat_axis=1, tiled=True)]
  transfers between devices with their start and end apart: 7 -> 30, of which waited for: 4 -> 17; matrix products, arithmetic and copies ran while one was open for 9% -> 1% of each run, Pallas kernels for 0% -> 15%
where the time goes in v1:
time: 289 us; the launch traced here: 287 us
  waiting for transfers between devices  146 us (51%)
  starting transfers between devices  60 us (21%)
  Pallas kernels  46.7 us (16%)
  local copies, waits for them, and re-layouts  27.7 us (10%)
  other arithmetic  5.72 us (2%)
    all_to_all x4, waiting for transfers between devices, exchange(): lax.all_to_all(rows, 'group', split_axis=0, concat_axis=0, tiled=True)  83.8 us
    ppermute x21, waiting for transfers between devices, along(): return lax.ppermute(shard, 'ingroup', hop)  61.5 us
    ppermute x21, starting transfers between devices, along(): return lax.ppermute(shard, 'ingroup', hop)  35.2 us
    unnamed x72, local copies, waits for them, and re-layouts  26.3 us
    all_to_all x4, starting transfers between devices, exchange(): lax.all_to_all(rows, 'group', split_axis=0, concat_axis=0, tiled=True)  23.7 us
    pallas_call x2, Pallas kernels, hidden_rows(): call(functools.partial(hidden_kernel, groups=groups, members=members, slo...  19.3 us
    pallas_call x1, Pallas kernels, down_first(): call(functools.partial(down_first_kernel, parts=len(hiddens), groups=grou...  8.62 us
    pallas_call x2, Pallas kernels, pick_rows(): call(functools.partial(pick_rows_kernel, groups=groups, per_group=per_gro...  6.71 us
  transfers between devices with their start and end apart: 30, of which 17 were waited for; matrix products, arithmetic and copies ran while one was open for 1% of the time, Pallas kernels for 15%

profile of v1, /device:TPU:8, one launch (start us, length us, event | category | flops | bytes accessed | tf_op | source)
XLA Modules:
  0.0 287.0 jit_solution(7822526620326360114)
XLA Ops:
  2.4 1.1 concatenate.10.refs_0_
  3.5 2.0 collective-permute-start
  5.5 4.0 %collective-permute-start.1 = (bf16[64,3712]{1,0:T(8,128)(2,1)S(1)}, bf16[64,3712]{1,0:T(8,128)(2,1)S(1)}, u32[]{:S(2)}, u32[]{:S(2)}) collective-permute-start(bf16[64,3712]{1,0:T(8,128)(2,1)S(1)} %concatenate.10.refs_0_), channel_id=1, source_target_pairs={{0,14},{1,15},{2,0},{3,1},{4,2},{5,3},{6,4},{7,5},{8,6},{9,7},{10,... | collective-permute-start | bytes 1425416 | tf_op jit(solution)/shard_map/ppermute | solution.py:334
  9.5 10.8 %collective-permute-done.refs_1_ = bf16[64,3712]{1,0:T(8,128)(2,1)S(1)} collective-permute-done((bf16[64,3712]{1,0:T(8,128)(2,1)S(1)}, bf16[64,3712]{1,0:T(8,128)(2,1)S(1)}, u32[]{:S(2)}, u32[]{:S(2)}) %collective-permute-start) | collective-permute-done | bytes 475168 | tf_op jit(solution)/shard_map/ppermute | solution.py:334
  20.4 13.2 %collective-permute-done.2.refs_3_ = bf16[64,3712]{1,0:T(8,128)(2,1)S(1)} collective-permute-done((bf16[64,3712]{1,0:T(8,128)(2,1)S(1)}, bf16[64,3712]{1,0:T(8,128)(2,1)S(1)}, u32[]{:S(2)}, u32[]{:S(2)}) %collective-permute-start.2) | collective-permute-done | bytes 475168 | tf_op jit(solution)/shard_map/ppermute | solution.py:334
  33.6 3.4 %pick_rows.2 = bf16[384,3712]{1,0:T(8,128)(2,1)} custom-call(s32[2]{0:T(128)S(1)} %pad_add_fusion.place_ref, bf16[64,3712]{1,0:T(8,128)(2,1)S(1)} %concatenate.10.refs_0_, bf16[64,3712]{1,0:T(8,128)(2,1)S(1)} %collective-permute-done.refs_1_, bf16[64,3712]{1,0:T(8,128)(2,1)S(1)} %collective-permute-done.1.refs_2_, ...), custom_call_target="tpu_custom_call" | custom-call | flops 729808896 | bytes 4751360 | tf_op jit(solution)/shard_map/pick_rows/pallas_call | solution.py:76
  37.0 7.4 %all-to-all-start = ((bf16[16,24,3712]{2,1,0:T(8,128)(2,1)}), bf16[16,24,3712]{2,1,0:T(8,128)(2,1)S(1)}, u32[]{:S(2)}, u32[]{:S(2)}) async-start(bf16[16,24,3712]{2,1,0:T(8,128)(2,1)} %bitcast.3), calls=%async_computation | async-start | bytes 5701632 | tf_op jit(solution)/shard_map/all_to_all | solution.py:340
  45.1 1.8 collective-permute-start.4
  46.9 11.1 %collective-permute-done.3.refs_4_.refs_0_ = bf16[64,3712]{1,0:T(8,128)(2,1)S(1)} collective-permute-done((bf16[64,3712]{1,0:T(8,128)(2,1)}, bf16[64,3712]{1,0:T(8,128)(2,1)S(1)}, u32[]{:S(2)}, u32[]{:S(2)}) %collective-permute-start.3) | collective-permute-done | bytes 475168 | tf_op jit(solution)/shard_map/ppermute | solution.py:334
  58.0 1.5 collective-permute-start.5
  60.0 10.0 %collective-permute-done.5.refs_6_.refs_2_ = bf16[64,3712]{1,0:T(8,128)(2,1)S(1)} collective-permute-done((bf16[64,3712]{1,0:T(8,128)(2,1)S(1)}, bf16[64,3712]{1,0:T(8,128)(2,1)S(1)}, u32[]{:S(2)}, u32[]{:S(2)}) %collective-permute-start.5) | collective-permute-done | bytes 475168 | tf_op jit(solution)/shard_map/ppermute | solution.py:334
  70.0 2.5 collective-permute-done.6.refs_7_.refs_3_
  72.5 3.3 %pick_rows.3 = bf16[384,3712]{1,0:T(8,128)(2,1)} custom-call(s32[2]{0:T(128)S(1)} %pad_add_fusion.place_ref, bf16[64,3712]{1,0:T(8,128)(2,1)S(1)} %collective-permute-done.3.refs_4_.refs_0_, bf16[64,3712]{1,0:T(8,128)(2,1)S(1)} %collective-permute-done.4.refs_5_.refs_1_, bf16[64,3712]{1,0:T(8,128)(2,1)S(1)} %collective-permute-done.5.refs_6_.refs_2_, ...), custom_call_target="tpu_custom_call" | custom-call | flops 729808896 | bytes 4751360 | tf_op jit(solution)/shard_map/pick_rows/pallas_call | solution.py:76
  79.0 2.6 all-to-all-done
  81.6 5.7 %all-to-all-start.1 = ((bf16[16,24,3712]{2,1,0:T(8,128)(2,1)}), bf16[16,24,3712]{2,1,0:T(8,128)(2,1)}, u32[]{:S(2)}, u32[]{:S(2)}) async-start(bf16[16,24,3712]{2,1,0:T(8,128)(2,1)} %bitcast.5), calls=%async_computation.1 | async-start | bytes 5701632 | tf_op jit(solution)/shard_map/all_to_all | solution.py:340
  87.3 2.0 copy-done.27
  89.3 9.1 %hidden_rows.2 = (bf16[384,1024]{1,0:T(8,128)(2,1)S(1)}, f32[8,384]{1,0:T(8,128)S(1)}, f32[384,128]{1,0:T(8,128)S(1)}) custom-call(s32[2]{0:T(128)S(1)} %pad_add_fusion.place_ref, bf16[384,3712]{1,0:T(8,128)(2,1)S(1)} %bitcast.14, bf16[1,1792,1024]{2,1,0:T(8,128)(2,1)S(1)} %copy-done.27, bf16[1,1792,1024]{2,1,0:T(8,128)(2,1)} %collective-permute-done.7.gate_other, ...), custom_call_target="tpu_custom_call" | custom-call | flops 5637144576 | bytes 18317312 | tf_op jit(solution)/shard_map/hidden_rows/pallas_call | solution.py:187
  100.5 25.1 %all-to-all-done.1 = bf16[16,24,3712]{2,1,0:T(8,128)(2,1)} async-done(((bf16[16,24,3712]{2,1,0:T(8,128)(2,1)}), bf16[16,24,3712]{2,1,0:T(8,128)(2,1)}, u32[]{:S(2)}, u32[]{:S(2)}) %all-to-all-start.1) | async-done | bytes 2850848 | tf_op jit(solution)/shard_map/all_to_all | solution.py:340
  125.7 2.0 copy-done.28
  127.7 10.1 %hidden_rows.3 = (bf16[384,1024]{1,0:T(8,128)(2,1)S(1)}, f32[8,384]{1,0:T(8,128)S(1)}, f32[384,128]{1,0:T(8,128)S(1)}) custom-call(s32[2]{0:T(128)S(1)} %pad_add_fusion.place_ref, bf16[384,3712]{1,0:T(8,128)(2,1)} %bitcast.6.rows_ref, bf16[1,1792,1024]{2,1,0:T(8,128)(2,1)S(1)} %copy-done.28, bf16[1,1792,1024]{2,1,0:T(8,128)(2,1)} %collective-permute-done.7.gate_other, ...), custom_call_target="tpu_custom_call" | custom-call | flops 5637144576 | bytes 18317312 | tf_op jit(solution)/shard_map/hidden_rows/pallas_call | solution.py:187
  138.0 1.2 collective-permute-done.10.refs_3_
  139.1 8.6 %down_first.1 = (bf16[768,1792]{1,0:T(8,128)(2,1)}, bf16[768,1024]{1,0:T(8,128)(2,1)S(1)}, bf16[768,128]{1,0:T(8,128)(2,1)S(1)}) custom-call(f32[8,384]{1,0:T(8,128)S(1)} %get-tuple-element.30.refs_0_, f32[8,384]{1,0:T(8,128)S(1)} %get-tuple-element.31.refs_1_, f32[8,384]{1,0:T(8,128)S(1)} %collective-permute-done.9.refs_2_, ...), custom_call_target="tpu_custom_call" | custom-call | flops 2818572288 | bytes 7995392 | tf_op jit(solution)/shard_map/down_first/pallas_call | solution.py:253
  147.8 1.2 copy-done.30
  148.9 5.0 %all-to-all-start.2 = ((bf16[16,48,1792]{2,1,0:T(8,128)(2,1)}), bf16[16,48,1792]{2,1,0:T(8,128)(2,1)S(1)}, u32[]{:S(2)}, u32[]{:S(2)}) async-start(bf16[16,48,1792]{2,1,0:T(8,128)(2,1)} %bitcast.16), calls=%async_computation.2 | async-start | bytes 5505024 | tf_op jit(solution)/shard_map/all_to_all | solution.py:340
  153.9 1.4 copy-done.31
  155.3 6.1 %down_second.1 = bf16[768,1920]{1,0:T(8,128)(2,1)S(1)} custom-call(bf16[768,1024]{1,0:T(8,128)(2,1)S(1)} %copy-done.31, bf16[768,128]{1,0:T(8,128)(2,1)S(1)} %get-tuple-element.46.flag_ref, bf16[1,1024,1792]{2,1,0:T(8,128)(2,1)} %collective-permute-done.18.weight_ref), custom_call_target="tpu_custom_call" | custom-call | flops 2818572288 | bytes 7995392 | tf_op jit(solution)/shard_map/down_second/pallas_call | solution.py:280
  161.5 1.5 copy-done
  163.0 33.0 %all-to-all-done.2 = bf16[16,48,1792]{2,1,0:T(8,128)(2,1)S(1)} async-done(((bf16[16,48,1792]{2,1,0:T(8,128)(2,1)}), bf16[16,48,1792]{2,1,0:T(8,128)(2,1)S(1)}, u32[]{:S(2)}, u32[]{:S(2)}) %all-to-all-start.2) | async-done | bytes 2752544 | tf_op jit(solution)/shard_map/all_to_all | solution.py:340
  196.0 1.6 copy-done.1
  197.6 5.6 %all-to-all-start.3 = ((bf16[16,48,1920]{2,1,0:T(8,128)(2,1)}), bf16[16,48,1920]{2,1,0:T(8,128)(2,1)S(1)}, u32[]{:S(2)}, u32[]{:S(2)}) async-start(bf16[16,48,1920]{2,1,0:T(8,128)(2,1)} %bitcast.13), calls=%async_computation.3 | async-start | bytes 5898240 | tf_op jit(solution)/shard_map/all_to_all | solution.py:340
  204.3 1.0 copy-done.6
  210.4 2.0 score_table.1.table_ref
  212.4 2.3 combine.2
  218.1 3.2 %collective-permute-start.11 = (bf16[64,1792]{1,0:T(8,128)(2,1)}, bf16[64,1792]{1,0:T(8,128)(2,1)}, u32[]{:S(2)}, u32[]{:S(2)}) collective-permute-start(bf16[64,1792]{1,0:T(8,128)(2,1)} %copy-done.29), channel_id=1, source_target_pairs={{0,14},{1,15},{2,0},{3,1},{4,2},{5,3},{6,4},{7,5},{8,6},{9,7},{10,... | collective-permute-start | bytes 688136 | tf_op jit(solution)/shard_map/ppermute | solution.py:334
  221.4 23.1 %all-to-all-done.3 = bf16[16,48,1920]{2,1,0:T(8,128)(2,1)S(1)} async-done(((bf16[16,48,1920]{2,1,0:T(8,128)(2,1)}), bf16[16,48,1920]{2,1,0:T(8,128)(2,1)S(1)}, u32[]{:S(2)}, u32[]{:S(2)}) %all-to-all-start.3) | async-done | bytes 2949152 | tf_op jit(solution)/shard_map/all_to_all | solution.py:340
  244.5 1.1 copy-done.18
  245.6 1.8 combine.3
  247.5 3.2 %collective-permute-start.19 = (bf16[64,1920]{1,0:T(8,128)(2,1)S(1)}, bf16[64,1920]{1,0:T(8,128)(2,1)S(1)}, u32[]{:S(2)}, u32[]{:S(2)}) collective-permute-start(bf16[64,1920]{1,0:T(8,128)(2,1)S(1)} %get-tuple-element.48), channel_id=1, source_target_pairs={{0,14},{1,15},{2,0},{3,1},{4,2},{5,3},{6,4},{7,5},{8,6},{9,7},{10,... | collective-permute-start | bytes 737288 | tf_op jit(solution)/shard_map/ppermute | solution.py:334
  252.9 3.5 %collective-permute-start.12 = (bf16[64,1792]{1,0:T(8,128)(2,1)S(1)}, bf16[64,1792]{1,0:T(8,128)(2,1)S(1)}, u32[]{:S(2)}, u32[]{:S(2)}) collective-permute-start(bf16[64,1792]{1,0:T(8,128)(2,1)S(1)} %add_convert_fusion.9), channel_id=1, source_target_pairs={{0,14},{1,15},{2,0},{3,1},{4,2},{5,3},{6,4},{7,5},{8,6},{9,7},{10,... | collective-permute-start | bytes 688136 | tf_op jit(solution)/shard_map/ppermute | solution.py:334
  256.8 3.3 %collective-permute-start.20 = (bf16[64,1920]{1,0:T(8,128)(2,1)S(1)}, bf16[64,1920]{1,0:T(8,128)(2,1)S(1)}, u32[]{:S(2)}, u32[]{:S(2)}) collective-permute-start(bf16[64,1920]{1,0:T(8,128)(2,1)S(1)} %add_convert_fusion.4), channel_id=1, source_target_pairs={{0,14},{1,15},{2,0},{3,1},{4,2},{5,3},{6,4},{7,5},{8,6},{9,7},{10,... | collective-permute-start | bytes 737288 | tf_op jit(solution)/shard_map/ppermute | solution.py:334
  260.1 1.5 collective-permute-done.16
  262.5 3.8 %collective-permute-start.13 = (bf16[64,1792]{1,0:T(8,128)(2,1)S(1)}, bf16[64,1792]{1,0:T(8,128)(2,1)S(1)}, u32[]{:S(2)}, u32[]{:S(2)}) collective-permute-start(bf16[64,1792]{1,0:T(8,128)(2,1)S(1)} %add_convert_fusion.8), channel_id=1, source_target_pairs={{0,14},{1,15},{2,0},{3,1},{4,2},{5,3},{6,4},{7,5},{8,6},{9,7},{10,... | collective-permute-start | bytes 688136 | tf_op jit(solution)/shard_map/ppermute | solution.py:334
  266.2 1.4 collective-permute-done.20
  267.7 3.8 %collective-permute-start.21 = (bf16[64,1920]{1,0:T(8,128)(2,1)S(1)}, bf16[64,1920]{1,0:T(8,128)(2,1)S(1)}, u32[]{:S(2)}, u32[]{:S(2)}) collective-permute-start(bf16[64,1920]{1,0:T(8,128)(2,1)S(1)} %add_convert_fusion.3), channel_id=1, source_target_pairs={{0,14},{1,15},{2,0},{3,1},{4,2},{5,3},{6,4},{7,5},{8,6},{9,7},{10,... | collective-permute-start | bytes 737288 | tf_op jit(solution)/shard_map/ppermute | solution.py:334
  271.7 3.6 %collective-permute-done.21 = bf16[64,1920]{1,0:T(8,128)(2,1)S(1)} collective-permute-done((bf16[64,1920]{1,0:T(8,128)(2,1)S(1)}, bf16[64,1920]{1,0:T(8,128)(2,1)S(1)}, u32[]{:S(2)}, u32[]{:S(2)}) %collective-permute-start.21) | collective-permute-done | bytes 245792 | tf_op jit(solution)/shard_map/ppermute | solution.py:334
  275.3 3.8 %collective-permute-start.22 = (bf16[64,1920]{1,0:T(8,128)(2,1)S(1)}, bf16[64,1920]{1,0:T(8,128)(2,1)S(1)}, u32[]{:S(2)}, u32[]{:S(2)}) collective-permute-start(bf16[64,1920]{1,0:T(8,128)(2,1)S(1)} %add_convert_fusion.2), channel_id=1, source_target_pairs={{0,14},{1,15},{2,0},{3,1},{4,2},{5,3},{6,4},{7,5},{8,6},{9,7},{10,... | collective-permute-start | bytes 737288 | tf_op jit(solution)/shard_map/ppermute | solution.py:334
  279.2 4.3 %collective-permute-done.22 = bf16[64,1920]{1,0:T(8,128)(2,1)S(1)} collective-permute-done((bf16[64,1920]{1,0:T(8,128)(2,1)S(1)}, bf16[64,1920]{1,0:T(8,128)(2,1)S(1)}, u32[]{:S(2)}, u32[]{:S(2)}) %collective-permute-start.22) | collective-permute-done | bytes 245792 | tf_op jit(solution)/shard_map/ppermute | solution.py:334
  283.8 2.3 collective-permute-done.14
  (117 shorter events, 23.7 us)
Async XLA Ops:
  3.5 16.8 %collective-permute-start = (bf16[64,3712]{1,0:T(8,128)(2,1)S(1)}, bf16[64,3712]{1,0:T(8,128)(2,1)S(1)}, u32[]{:S(2)}, u32[]{:S(2)}) collective-permute-start(bf16[64,3712]{1,0:T(8,128)(2,1)S(1)} %concatenate.10.refs_0_), channel_id=1, source_target_pairs={{0,2},{1,3},{2,4},{3,5},{4,6},{5,7},{6,8},{7,9},{8,10},{9,11},{10,... | collective-permute-start | bytes 1425416 | tf_op jit(solution)/shard_map/ppermute | solution.py:334
  5.5 14.9 %collective-permute-start.1 = (bf16[64,3712]{1,0:T(8,128)(2,1)S(1)}, bf16[64,3712]{1,0:T(8,128)(2,1)S(1)}, u32[]{:S(2)}, u32[]{:S(2)}) collective-permute-start(bf16[64,3712]{1,0:T(8,128)(2,1)S(1)} %concatenate.10.refs_0_), channel_id=1, source_target_pairs={{0,14},{1,15},{2,0},{3,1},{4,2},{5,3},{6,4},{7,5},{8,6},{9,7},{10,... | collective-permute-start | bytes 1425416 | tf_op jit(solution)/shard_map/ppermute | solution.py:334
  20.3 16.6 %copy-start.3 = (bf16[64,3712]{1,0:T(8,128)(2,1)}, bf16[64,3712]{1,0:T(8,128)(2,1)S(1)}, u32[]{:S(2)}) copy-start(bf16[64,3712]{1,0:T(8,128)(2,1)S(1)} %collective-permute-done.refs_1_) | copy-start | bytes 1425412
  20.3 13.3 %collective-permute-start.2 = (bf16[64,3712]{1,0:T(8,128)(2,1)S(1)}, bf16[64,3712]{1,0:T(8,128)(2,1)S(1)}, u32[]{:S(2)}, u32[]{:S(2)}) collective-permute-start(bf16[64,3712]{1,0:T(8,128)(2,1)S(1)} %collective-permute-done.refs_1_), channel_id=1, source_target_pairs={{0,2},{1,3},{2,4},{3,5},{4,6},{5,7},{6,8},{7,9},{8,10},{9,11},{10,... | collective-permute-start | bytes 1425416 | tf_op jit(solution)/shard_map/ppermute | solution.py:334
  20.4 16.6 %copy-start.5 = (bf16[64,3712]{1,0:T(8,128)(2,1)}, bf16[64,3712]{1,0:T(8,128)(2,1)S(1)}, u32[]{:S(2)}) copy-start(bf16[64,3712]{1,0:T(8,128)(2,1)S(1)} %collective-permute-done.1.refs_2_) | copy-start | bytes 1425412
  33.6 3.4 %copy-start.7 = (bf16[64,3712]{1,0:T(8,128)(2,1)}, bf16[64,3712]{1,0:T(8,128)(2,1)S(1)}, u32[]{:S(2)}) copy-start(bf16[64,3712]{1,0:T(8,128)(2,1)S(1)} %collective-permute-done.2.refs_3_) | copy-start | bytes 1425412
  37.0 44.6 %all-to-all-start = ((bf16[16,24,3712]{2,1,0:T(8,128)(2,1)}), bf16[16,24,3712]{2,1,0:T(8,128)(2,1)S(1)}, u32[]{:S(2)}, u32[]{:S(2)}) async-start(bf16[16,24,3712]{2,1,0:T(8,128)(2,1)} %bitcast.3), calls=%async_computation | async-start | bytes 5701632 | tf_op jit(solution)/shard_map/all_to_all | solution.py:340
  44.4 42.9 %collective-permute-start.7 = (bf16[1,1792,1024]{2,1,0:T(8,128)(2,1)}, bf16[1,1792,1024]{2,1,0:T(8,128)(2,1)}, u32[]{:S(2)}, u32[]{:S(2)}) collective-permute-start(bf16[1,1792,1024]{2,1,0:T(8,128)(2,1)} %gate_own.3), channel_id=1, source_target_pairs={{0,1},{1,0},{2,3},{3,2},{4,5},{5,4},{6,7},{7,6},{8,9},{9,8},{10,11... | collective-permute-start | bytes 11010056 | tf_op jit(solution)/shard_map/ppermute | solution.py:337
  44.4 42.9 %collective-permute-start.8 = (bf16[1,1792,1024]{2,1,0:T(8,128)(2,1)}, bf16[1,1792,1024]{2,1,0:T(8,128)(2,1)}, u32[]{:S(2)}, u32[]{:S(2)}) collective-permute-start(bf16[1,1792,1024]{2,1,0:T(8,128)(2,1)} %up_own.3), channel_id=1, source_target_pairs={{0,1},{1,0},{2,3},{3,2},{4,5},{5,4},{6,7},{7,6},{8,9},{9,8},{10,11... | collective-permute-start | bytes 11010056 | tf_op jit(solution)/shard_map/ppermute | solution.py:337
  44.9 13.1 %collective-permute-start.3 = (bf16[64,3712]{1,0:T(8,128)(2,1)}, bf16[64,3712]{1,0:T(8,128)(2,1)S(1)}, u32[]{:S(2)}, u32[]{:S(2)}) collective-permute-start(bf16[64,3712]{1,0:T(8,128)(2,1)} %copy-done.5), channel_id=1, source_target_pairs={{0,14},{1,15},{2,0},{3,1},{4,2},{5,3},{6,4},{7,5},{8,6},{9,7},{10,... | collective-permute-start | bytes 1425416 | tf_op jit(solution)/shard_map/ppermute | solution.py:334
  45.1 14.4 %collective-permute-start.4 = (bf16[64,3712]{1,0:T(8,128)(2,1)}, bf16[64,3712]{1,0:T(8,128)(2,1)S(1)}, u32[]{:S(2)}, u32[]{:S(2)}) collective-permute-start(bf16[64,3712]{1,0:T(8,128)(2,1)} %copy-done.7), channel_id=1, source_target_pairs={{0,2},{1,3},{2,4},{3,5},{4,6},{5,7},{6,8},{7,9},{8,10},{9,11},{10,... | collective-permute-start | bytes 1425416 | tf_op jit(solution)/shard_map/ppermute | solution.py:334
  58.0 12.0 %collective-permute-start.5 = (bf16[64,3712]{1,0:T(8,128)(2,1)S(1)}, bf16[64,3712]{1,0:T(8,128)(2,1)S(1)}, u32[]{:S(2)}, u32[]{:S(2)}) collective-permute-start(bf16[64,3712]{1,0:T(8,128)(2,1)S(1)} %collective-permute-done.3.refs_4_.refs_0_), channel_id=1, source_target_pairs={{0,14},{1,15},{2,0},{3,1},{4,2},{5,3},{6,4},{7,5},{8,6},{9,7},{10,... | collective-permute-start | bytes 1425416 | tf_op jit(solution)/shard_map/ppermute | solution.py:334
  59.5 13.1 %collective-permute-start.6 = (bf16[64,3712]{1,0:T(8,128)(2,1)S(1)}, bf16[64,3712]{1,0:T(8,128)(2,1)S(1)}, u32[]{:S(2)}, u32[]{:S(2)}) collective-permute-start(bf16[64,3712]{1,0:T(8,128)(2,1)S(1)} %collective-permute-done.4.refs_5_.refs_1_), channel_id=1, source_target_pairs={{0,2},{1,3},{2,4},{3,5},{4,6},{5,7},{6,8},{7,9},{8,10},{9,11},{10,... | collective-permute-start | bytes 1425416 | tf_op jit(solution)/shard_map/ppermute | solution.py:334
  81.6 44.1 %all-to-all-start.1 = ((bf16[16,24,3712]{2,1,0:T(8,128)(2,1)}), bf16[16,24,3712]{2,1,0:T(8,128)(2,1)}, u32[]{:S(2)}, u32[]{:S(2)}) async-start(bf16[16,24,3712]{2,1,0:T(8,128)(2,1)} %bitcast.5), calls=%async_computation.1 | async-start | bytes 5701632 | tf_op jit(solution)/shard_map/all_to_all | solution.py:340
  87.3 66.7 %collective-permute-start.18 = (bf16[1,1024,1792]{2,1,0:T(8,128)(2,1)}, bf16[1,1024,1792]{2,1,0:T(8,128)(2,1)}, u32[]{:S(2)}, u32[]{:S(2)}) collective-permute-start(bf16[1,1024,1792]{2,1,0:T(8,128)(2,1)} %refs_8_.1), channel_id=1, source_target_pairs={{0,1},{1,0},{2,3},{3,2},{4,5},{5,4},{6,7},{7,6},{8,9},{9,8},{10,11... | collective-permute-start | bytes 11010056 | tf_op jit(solution)/shard_map/ppermute | solution.py:337
  87.3 2.0 copy-start.27
  100.1 37.9 %collective-permute-start.9 = (f32[8,384]{1,0:T(8,128)S(1)}, f32[8,384]{1,0:T(8,128)S(1)}, u32[]{:S(2)}, u32[]{:S(2)}) collective-permute-start(f32[8,384]{1,0:T(8,128)S(1)} %get-tuple-element.30.refs_0_), channel_id=1, source_target_pairs={{0,1},{1,0},{2,3},{3,2},{4,5},{5,4},{6,7},{7,6},{8,9},{9,8},{10,11... | collective-permute-start | bytes 36872 | tf_op jit(solution)/shard_map/ppermute | solution.py:337
  125.7 2.0 copy-start.28
  127.7 11.4 %copy-start.33 = (bf16[384,1024]{1,0:T(8,128)(2,1)S(1)}, bf16[384,1024]{1,0:T(8,128)(2,1)}, u32[]{:S(2)}) copy-start(bf16[384,1024]{1,0:T(8,128)(2,1)} %copy-done.32) | copy-start | bytes 2359300
  127.7 11.4 %copy-start.35 = (f32[384,128]{1,0:T(8,128)S(1)}, f32[384,128]{1,0:T(8,128)}, u32[]{:S(2)}) copy-start(f32[384,128]{1,0:T(8,128)} %copy-done.34) | copy-start | bytes 589828
  137.9 1.3 collective-permute-start.10
  147.7 1.2 copy-start.30
  148.9 47.1 %all-to-all-start.2 = ((bf16[16,48,1792]{2,1,0:T(8,128)(2,1)}), bf16[16,48,1792]{2,1,0:T(8,128)(2,1)S(1)}, u32[]{:S(2)}, u32[]{:S(2)}) async-start(bf16[16,48,1792]{2,1,0:T(8,128)(2,1)} %bitcast.16), calls=%async_computation.2 | async-start | bytes 5505024 | tf_op jit(solution)/shard_map/all_to_all | solution.py:340
  153.9 1.4 copy-start.31
  161.5 1.6 copy-start
  196.0 1.6 copy-start.1
  197.6 46.9 %all-to-all-start.3 = ((bf16[16,48,1920]{2,1,0:T(8,128)(2,1)}), bf16[16,48,1920]{2,1,0:T(8,128)(2,1)S(1)}, u32[]{:S(2)}, u32[]{:S(2)}) async-start(bf16[16,48,1920]{2,1,0:T(8,128)(2,1)} %bitcast.13), calls=%async_computation.3 | async-start | bytes 5898240 | tf_op jit(solution)/shard_map/all_to_all | solution.py:340
  210.4 2.0 copy-start.2
  212.4 2.3 copy-start.17
  218.1 32.6 %collective-permute-start.15 = (bf16[64,1792]{1,0:T(8,128)(2,1)}, bf16[64,1792]{1,0:T(8,128)(2,1)}, u32[]{:S(2)}, u32[]{:S(2)}) collective-permute-start(bf16[64,1792]{1,0:T(8,128)(2,1)} %get-tuple-element.42), channel_id=1, source_target_pairs={{0,2},{1,3},{2,4},{3,5},{4,6},{5,7},{6,8},{7,9},{8,10},{9,11},{10,... | collective-permute-start | bytes 688136 | tf_op jit(solution)/shard_map/ppermute | solution.py:334
  218.1 33.7 %collective-permute-start.11 = (bf16[64,1792]{1,0:T(8,128)(2,1)}, bf16[64,1792]{1,0:T(8,128)(2,1)}, u32[]{:S(2)}, u32[]{:S(2)}) collective-permute-start(bf16[64,1792]{1,0:T(8,128)(2,1)} %copy-done.29), channel_id=1, source_target_pairs={{0,14},{1,15},{2,0},{3,1},{4,2},{5,3},{6,4},{7,5},{8,6},{9,7},{10,... | collective-permute-start | bytes 688136 | tf_op jit(solution)/shard_map/ppermute | solution.py:334
  244.5 1.1 copy-start.18
  245.6 5.2 %copy-start.26 = (bf16[64,1792]{1,0:T(8,128)(2,1)S(1)}, bf16[64,1792]{1,0:T(8,128)(2,1)}, u32[]{:S(2)}) copy-start(bf16[64,1792]{1,0:T(8,128)(2,1)} %copy-done.25) | copy-start | bytes 688132
  245.6 6.3 %copy-start.24 = (bf16[64,1792]{1,0:T(8,128)(2,1)S(1)}, bf16[64,1792]{1,0:T(8,128)(2,1)}, u32[]{:S(2)}) copy-start(bf16[64,1792]{1,0:T(8,128)(2,1)} %copy-done.23) | copy-start | bytes 688132
  245.6 16.0 %copy-start.22 = (bf16[64,1792]{1,0:T(8,128)(2,1)S(1)}, bf16[64,1792]{1,0:T(8,128)(2,1)}, u32[]{:S(2)}) copy-start(bf16[64,1792]{1,0:T(8,128)(2,1)} %copy-done.21) | copy-start | bytes 688132
  247.4 15.0 %copy-start.20 = (bf16[64,1792]{1,0:T(8,128)(2,1)S(1)}, bf16[64,1792]{1,0:T(8,128)(2,1)}, u32[]{:S(2)}) copy-start(bf16[64,1792]{1,0:T(8,128)(2,1)} %copy-done.19) | copy-start | bytes 688132
  247.4 9.1 %collective-permute-start.23 = (bf16[64,1920]{1,0:T(8,128)(2,1)S(1)}, bf16[64,1920]{1,0:T(8,128)(2,1)S(1)}, u32[]{:S(2)}, u32[]{:S(2)}) collective-permute-start(bf16[64,1920]{1,0:T(8,128)(2,1)S(1)} %get-tuple-element.52), channel_id=1, source_target_pairs={{0,2},{1,3},{2,4},{3,5},{4,6},{5,7},{6,8},{7,9},{8,10},{9,11},{10,... | collective-permute-start | bytes 737288 | tf_op jit(solution)/shard_map/ppermute | solution.py:334
  247.5 9.2 %collective-permute-start.19 = (bf16[64,1920]{1,0:T(8,128)(2,1)S(1)}, bf16[64,1920]{1,0:T(8,128)(2,1)S(1)}, u32[]{:S(2)}, u32[]{:S(2)}) collective-permute-start(bf16[64,1920]{1,0:T(8,128)(2,1)S(1)} %get-tuple-element.48), channel_id=1, source_target_pairs={{0,14},{1,15},{2,0},{3,1},{4,2},{5,3},{6,4},{7,5},{8,6},{9,7},{10,... | collective-permute-start | bytes 737288 | tf_op jit(solution)/shard_map/ppermute | solution.py:334
  251.7 9.8 %collective-permute-start.16 = (bf16[64,1792]{1,0:T(8,128)(2,1)S(1)}, bf16[64,1792]{1,0:T(8,128)(2,1)S(1)}, u32[]{:S(2)}, u32[]{:S(2)}) collective-permute-start(bf16[64,1792]{1,0:T(8,128)(2,1)S(1)} %add_convert_fusion.6), channel_id=1, source_target_pairs={{0,2},{1,3},{2,4},{3,5},{4,6},{5,7},{6,8},{7,9},{8,10},{9,11},{10,... | collective-permute-start | bytes 688136 | tf_op jit(solution)/shard_map/ppermute | solution.py:334
  252.9 9.6 %collective-permute-start.12 = (bf16[64,1792]{1,0:T(8,128)(2,1)S(1)}, bf16[64,1792]{1,0:T(8,128)(2,1)S(1)}, u32[]{:S(2)}, u32[]{:S(2)}) collective-permute-start(bf16[64,1792]{1,0:T(8,128)(2,1)S(1)} %add_convert_fusion.9), channel_id=1, source_target_pairs={{0,14},{1,15},{2,0},{3,1},{4,2},{5,3},{6,4},{7,5},{8,6},{9,7},{10,... | collective-permute-start | bytes 688136 | tf_op jit(solution)/shard_map/ppermute | solution.py:334
  256.6 14.9 %collective-permute-start.24 = (bf16[64,1920]{1,0:T(8,128)(2,1)S(1)}, bf16[64,1920]{1,0:T(8,128)(2,1)S(1)}, u32[]{:S(2)}, u32[]{:S(2)}) collective-permute-start(bf16[64,1920]{1,0:T(8,128)(2,1)S(1)} %add_convert_fusion.1), channel_id=1, source_target_pairs={{0,2},{1,3},{2,4},{3,5},{4,6},{5,7},{6,8},{7,9},{8,10},{9,11},{10,... | collective-permute-start | bytes 737288 | tf_op jit(solution)/shard_map/ppermute | solution.py:334
  256.8 10.9 %collective-permute-start.20 = (bf16[64,1920]{1,0:T(8,128)(2,1)S(1)}, bf16[64,1920]{1,0:T(8,128)(2,1)S(1)}, u32[]{:S(2)}, u32[]{:S(2)}) collective-permute-start(bf16[64,1920]{1,0:T(8,128)(2,1)S(1)} %add_convert_fusion.4), channel_id=1, source_target_pairs={{0,14},{1,15},{2,0},{3,1},{4,2},{5,3},{6,4},{7,5},{8,6},{9,7},{10,... | collective-permute-start | bytes 737288 | tf_op jit(solution)/shard_map/ppermute | solution.py:334
  261.6 22.1 %collective-permute-start.17 = (bf16[64,1792]{1,0:T(8,128)(2,1)S(1)}, bf16[64,1792]{1,0:T(8,128)(2,1)S(1)}, u32[]{:S(2)}, u32[]{:S(2)}) collective-permute-start(bf16[64,1792]{1,0:T(8,128)(2,1)S(1)} %add_convert_fusion.5), channel_id=1, source_target_pairs={{0,2},{1,3},{2,4},{3,5},{4,6},{5,7},{6,8},{7,9},{8,10},{9,11},{10,... | collective-permute-start | bytes 688136 | tf_op jit(solution)/shard_map/ppermute | solution.py:334
  262.5 16.6 %collective-permute-start.13 = (bf16[64,1792]{1,0:T(8,128)(2,1)S(1)}, bf16[64,1792]{1,0:T(8,128)(2,1)S(1)}, u32[]{:S(2)}, u32[]{:S(2)}) collective-permute-start(bf16[64,1792]{1,0:T(8,128)(2,1)S(1)} %add_convert_fusion.8), channel_id=1, source_target_pairs={{0,14},{1,15},{2,0},{3,1},{4,2},{5,3},{6,4},{7,5},{8,6},{9,7},{10,... | collective-permute-start | bytes 688136 | tf_op jit(solution)/shard_map/ppermute | solution.py:334
  267.7 7.5 %collective-permute-start.21 = (bf16[64,1920]{1,0:T(8,128)(2,1)S(1)}, bf16[64,1920]{1,0:T(8,128)(2,1)S(1)}, u32[]{:S(2)}, u32[]{:S(2)}) collective-permute-start(bf16[64,1920]{1,0:T(8,128)(2,1)S(1)} %add_convert_fusion.3), channel_id=1, source_target_pairs={{0,14},{1,15},{2,0},{3,1},{4,2},{5,3},{6,4},{7,5},{8,6},{9,7},{10,... | collective-permute-start | bytes 737288 | tf_op jit(solution)/shard_map/ppermute | solution.py:334
  271.6 7.6 %collective-permute-start.25 = (bf16[64,1920]{1,0:T(8,128)(2,1)S(1)}, bf16[64,1920]{1,0:T(8,128)(2,1)S(1)}, u32[]{:S(2)}, u32[]{:S(2)}) collective-permute-start(bf16[64,1920]{1,0:T(8,128)(2,1)S(1)} %add_convert_fusion), channel_id=1, source_target_pairs={{0,2},{1,3},{2,4},{3,5},{4,6},{5,7},{6,8},{7,9},{8,10},{9,11},{10,... | collective-permute-start | bytes 737288 | tf_op jit(solution)/shard_map/ppermute | solution.py:334
  275.3 8.3 %collective-permute-start.22 = (bf16[64,1920]{1,0:T(8,128)(2,1)S(1)}, bf16[64,1920]{1,0:T(8,128)(2,1)S(1)}, u32[]{:S(2)}, u32[]{:S(2)}) collective-permute-start(bf16[64,1920]{1,0:T(8,128)(2,1)S(1)} %add_convert_fusion.2), channel_id=1, source_target_pairs={{0,14},{1,15},{2,0},{3,1},{4,2},{5,3},{6,4},{7,5},{8,6},{9,7},{10,... | collective-permute-start | bytes 737288 | tf_op jit(solution)/shard_map/ppermute | solution.py:334
  279.1 6.9 %collective-permute-start.14 = (bf16[64,1792]{1,0:T(8,128)(2,1)S(1)}, bf16[64,1792]{1,0:T(8,128)(2,1)S(1)}, u32[]{:S(2)}, u32[]{:S(2)}) collective-permute-start(bf16[64,1792]{1,0:T(8,128)(2,1)S(1)} %add_convert_fusion.7), channel_id=1, source_target_pairs={{0,14},{1,15},{2,0},{3,1},{4,2},{5,3},{6,4},{7,5},{8,6},{9,7},{10,... | collective-permute-start | bytes 688136 | tf_op jit(solution)/shard_map/ppermute | solution.py:334
  (18 other events, 15.3 us)

commit v2 on v1

v2 whole, which is shorter than its diff:
```python
import functools

import jax
import jax.numpy as jnp
from jax import lax
from jax.experimental import pallas as pl
from jax.experimental.pallas import tpu as pltpu
from jax.sharding import PartitionSpec as P

TOPG = 4
META = 128
AT_SCORE, AT_POS, AT_ONE = 8, 16, 17
EMPTY = 1.0e9
NEAR = (0, -1, 1, -2)
FAR = (2, -3, 3, -4)
F32, BF16 = jnp.float32, jnp.bfloat16


def iota(shape, axis):
    return lax.broadcasted_iota(jnp.int32, shape, axis)


def divided(value, by, most):
    total = jnp.zeros_like(value)
    for j in range(1, most):
        total = total + (value >= j * by).astype(jnp.int32)
    return total


def tiles(width, tile):
    return [(at, min(tile, width - at)) for at in range(0, width, tile)]


def call(kernel, name, out_shape, flops, moved, vmem, **more):
    return pl.pallas_call(
        kernel,
        out_shape=out_shape,
        name=name,
        cost_estimate=pl.CostEstimate(flops=flops, bytes_accessed=moved, transcendentals=0),
        compiler_params=pltpu.CompilerParams(vmem_limit_bytes=vmem << 20),
        **more,
    )


WHOLE = pl.BlockSpec(memory_space=pltpu.VMEM)
SCALARS = pl.BlockSpec(memory_space=pltpu.SMEM)


STAYS = pl.BlockSpec(memory_space=pltpu.HBM)


def far_memory(*arrays):
    return [pltpu.with_memory_space_constraint(a, pltpu.HBM) for a in arrays]


def unit(rows):
    return (iota((rows, META), 0) == iota((rows, META), 1)).astype(F32).astype(BF16)


def lines_of(columns, rows):
    return lax.dot_general(
        unit(rows), columns, (((1,), (1,)), ((), ())), preferred_element_type=F32
    )


def start_rows_kernel(rows_ref, ids_ref, scores_ref, pos_ref, left_ref, right_ref):
    half = left_ref.shape[1]
    tok = rows_ref.shape[0]
    lines = [ids_ref[...].astype(F32), scores_ref[...].astype(F32), pos_ref[...].astype(F32)]
    lines.append(jnp.ones((1, tok), F32))
    lines.append(jnp.zeros((14, tok), F32))
    lines = jnp.concatenate(lines, axis=0).astype(BF16)
    meta = lax.dot_general(lines, unit(32), (((0,), (0,)), ((), ())), preferred_element_type=F32)
    left_ref[...] = rows_ref[:, :half]
    right_ref[:, :half] = rows_ref[:, half:]
    right_ref[:, half:] = meta.astype(BF16)


def start_rows(rows, ids, scores, pos):
    tok, model = rows.shape
    half = model // 2
    return call(
        start_rows_kernel,
        "start_rows",
        (jax.ShapeDtypeStruct((tok, half), BF16), jax.ShapeDtypeStruct((tok, half + META), BF16)),
        0,
        4 * tok * model,
        4,
        grid=(1,),
        in_specs=[
            pl.BlockSpec(a.shape, lambda i: (0, 0)) for a in (rows, ids.T, scores.T, pos[None, :])
        ],
        out_specs=(
            pl.BlockSpec((tok, half), lambda i: (0, 0)),
            pl.BlockSpec((tok, half + META), lambda i: (0, 0)),
        ),
    )(*far_memory(rows, ids.T, scores.T, pos[None, :]))


def pick_rows_kernel(place_ref, *refs, groups, per_group, slots, first_block, first_row, rows):
    out_ref, meta_ref, built_ref, sent = refs[-4:]
    count = (len(refs) - 4) // 2
    lefts, rights = refs[:count], refs[count:-4]
    copies = []
    tok, half = lefts[0].shape
    total = tok * count
    meta = jnp.concatenate([b[:, half:] for b in rights], axis=0)
    meta_ref[...] = meta
    meta_t = lines_of(meta, 32)
    expert = (iota((groups, total), 0) * per_group + place_ref[0]).astype(F32)
    hit = jnp.zeros((groups, total), F32)
    for k in range(AT_SCORE):
        hit = hit + (meta_t[k : k + 1, :] == expert).astype(F32)
    first, second = iota((total, total), 0), iota((total, total), 1)
    same = divided(first, tok, count) == divided(second, tok, count)
    before = (same & (first < second)).astype(F32).astype(BF16)
    occurrence = jnp.dot(hit.astype(BF16), before, preferred_element_type=F32)
    block_of = divided(iota((groups, total), 1), tok, count).astype(F32)
    slot = occurrence + slots * (block_of + first_block) - first_row
    slot = jnp.where(hit > 0, slot, -1.0)
    slot = jnp.broadcast_to(slot[:, None, :], (groups, rows, total))
    chosen = (slot == iota((groups, rows, total), 1).astype(F32)).astype(F32)
    chosen = chosen.reshape(groups * rows, total).astype(BF16)
    for start, blocks in ((0, lefts), (half, rights)):
        for at, wide in tiles(blocks[0].shape[1], 512):
            part = jnp.concatenate([b[:, at : at + wide] for b in blocks], axis=0)
            cut = pl.ds(start + at, wide)
            built_ref[:, cut] = jnp.dot(chosen, part, preferred_element_type=F32).astype(BF16)
            copies.append(
                pltpu.make_async_copy(built_ref.at[:, cut], out_ref.at[:, cut], sent.at[len(copies)])
            )
            copies[-1].start()
    for copy in copies:
        copy.wait()


def pick_rows(place, lefts, rights, groups, per_group, slots, first_block, first_row, rows):
    width = lefts[0].shape[1] + rights[0].shape[1]
    total = lefts[0].shape[0] * len(lefts)
    return call(
        functools.partial(
            pick_rows_kernel, groups=groups, per_group=per_group, slots=slots,
            first_block=first_block, first_row=first_row, rows=rows,
        ),
        "pick_rows",
        (pltpu.HBM((groups * rows, width), BF16), jax.ShapeDtypeStruct((total, META), BF16)),
        2 * groups * rows * total * width,
        2 * (groups * rows + total) * width,
        12,
        in_specs=[SCALARS] + [WHOLE] * (2 * len(lefts)),
        out_specs=(STAYS, WHOLE),
        scratch_shapes=[pltpu.VMEM((groups * rows, width), BF16), pltpu.SemaphoreType.DMA((8,))],
    )(place, *lefts, *rights)


def score_table_kernel(place_ref, meta_ref, out_ref, *, groups, per_group, slots, blocks):
    total = meta_ref.shape[0]
    tok = total // blocks
    rows = slots * blocks
    meta = meta_ref[...].astype(F32)
    expert = (iota((total, META), 1) * per_group + place_ref[0]).astype(F32)
    hit = jnp.zeros((total, META), F32)
    score = jnp.zeros((total, META), F32)
    for k in range(AT_SCORE):
        same = (meta[:, k : k + 1] == expert).astype(F32)
        hit = hit + same
        score = score + same * meta[:, AT_SCORE + k : AT_SCORE + k + 1]
    first, second = iota((total, total), 0), iota((total, total), 1)
    same = divided(first, tok, blocks) == divided(second, tok, blocks)
    before = (same & (second < first)).astype(F32).astype(BF16)
    occurrence = jnp.dot(before, hit.astype(BF16), preferred_element_type=F32)
    block_of = divided(iota((total, META), 0), tok, blocks).astype(F32)
    slot = jnp.where(hit > 0, occurrence + slots * block_of, -1.0)
    source, lane = iota((META, groups * rows), 0), iota((META, groups * rows), 1)
    spread = ((lane >= source * rows) & (lane < source * rows + rows)).astype(F32).astype(BF16)
    slot_wide = jnp.dot(slot.astype(BF16), spread, preferred_element_type=F32)
    score_wide = jnp.dot(score.astype(BF16), spread, preferred_element_type=F32)
    column = iota((1, groups * rows), 1)
    column = (column - rows * divided(column, rows, groups)).astype(F32)
    out_ref[...] = jnp.where(slot_wide == column, score_wide, 0.0).astype(BF16)


def score_table(place, meta, groups, per_group, slots, blocks):
    total = meta.shape[0]
    columns = groups * slots * blocks
    return call(
        functools.partial(
            score_table_kernel, groups=groups, per_group=per_group, slots=slots, blocks=blocks
        ),
        "score_table",
        pltpu.HBM((total, columns), BF16),
        2 * total * columns * (2 * META),
        2 * total * columns,
        12,
        grid=(1,),
        in_specs=[SCALARS, pl.BlockSpec((total, META), lambda i: (0, 0))],
        out_specs=pl.BlockSpec((total, columns), lambda i: (0, 0)),
    )(place, meta)


def slot_keys_kernel(place_ref, *refs, groups, members, slots, offsets):
    meta_refs, (line_ref, column_ref) = refs[:-2], refs[-2:]
    z, c = place_ref[0], place_ref[1]
    rows = line_ref.shape[1] // groups
    first = 0
    for meta_ref in meta_refs:
        count = meta_ref.shape[0]
        part = count // groups
        meta = meta_ref[...]
        meta_t = lines_of(meta, 32)

        def key(index, position, valid):
            group = divided(index, part, groups)
            block = divided(index - part * group + first, slots, len(offsets))
            apart = jnp.zeros_like(index)
            for j, offset in enumerate(offsets):
                apart = apart + jnp.where(block == j, offset, 0)
            ring = members // 2
            where = z + apart
            where = jnp.where(where < 0, where + ring, where)
            where = jnp.where(where >= ring, where - ring, where)
            source = (group * members + where * 2 + c).astype(F32)
            return jnp.where(valid > 0, position * (groups * members) + source, EMPTY)

        line = key(iota((1, count), 1), meta_t[AT_POS : AT_POS + 1], meta_t[AT_ONE : AT_ONE + 1])
        at = first * groups
        line_ref[:, at : at + count] = jnp.broadcast_to(line, (line_ref.shape[0], count))
        wide = meta.astype(F32)
        column = key(
            iota((count, 1), 0), wide[:, AT_POS : AT_POS + 1], wide[:, AT_ONE : AT_ONE + 1]
        )
        column = jnp.broadcast_to(column, meta.shape)
        for g in range(groups):
            at = g * rows + first
            column_ref[at : at + part, :] = column[g * part : (g + 1) * part]
        first += part


def slot_keys(place, parts, groups, members, slots, offsets):
    count = sum(rows.shape[0] for rows in parts)
    last = parts[0].shape[1] // META - 1
    return call(
        functools.partial(
            slot_keys_kernel, groups=groups, members=members, slots=slots, offsets=offsets
        ),
        "slot_keys",
        (jax.ShapeDtypeStruct((8, count), F32), jax.ShapeDtypeStruct((count, META), F32)),
        0,
        16 * count * META,
        4,
        grid=(1,),
        in_specs=[SCALARS]
        + [pl.BlockSpec((rows.shape[0], META), lambda i: (0, last)) for rows in parts],
        out_specs=(
            pl.BlockSpec((8, count), lambda i: (0, 0)),
            pl.BlockSpec((count, META), lambda i: (0, 0)),
        ),
    )(place, *parts)


def kept_flags(lines, columns, capacity):
    count = columns[0].shape[0]
    lane = iota((count, META), 1)
    flags = jnp.zeros((count, META), F32)
    for q, column_ref in enumerate(columns):
        own = column_ref[:, :1]
        rank = jnp.zeros(own.shape, F32)
        for line_ref in lines:
            rank = rank + jnp.sum((line_ref[:1, :] < own).astype(F32), axis=1, keepdims=True)
        kept = jnp.where((rank < capacity) & (own < EMPTY), 1.0, 0.0)
        flags = jnp.where(lane == q, kept, flags)
    return flags.astype(BF16)


def expert_kernel(
    place_ref, gate_own, gate_other, up_own, up_other, down_own, down_other, *refs, lines, capacity
):
    line_refs, refs = refs[:lines], refs[lines:]
    column_refs, refs = refs[: lines // 2], refs[lines // 2 :]
    came_ref, out_ref, total_ref, rows_ref, came = refs
    half = gate_own.shape[1]
    c = place_ref[1]
    step = pl.program_id(0)

    @pl.when(step == 0)
    def _():
        copy = pltpu.make_async_copy(came_ref, rows_ref, came)
        copy.start()
        if lines:
            out_ref[:, 2 * half :] = kept_flags(line_refs, column_refs, capacity)
        copy.wait()

    own = rows_ref[:, pl.ds(pl.multiple_of(c * half, 128), half)]
    other = rows_ref[:, pl.ds(pl.multiple_of((1 - c) * half, 128), half)]
    gate = jnp.dot(own, gate_own[0], preferred_element_type=F32) + jnp.dot(
        other, gate_other[0], preferred_element_type=F32
    )
    up = jnp.dot(own, up_own[0], preferred_element_type=F32) + jnp.dot(
        other, up_other[0], preferred_element_type=F32
    )
    hidden = (gate / (1.0 + jnp.exp(-gate)) * up).astype(BF16)
    for at, down in ((0, down_own), (half, down_other)):
        part = jnp.dot(hidden, down[0], preferred_element_type=F32)
        cut = slice(at, at + half)

        @pl.when(step == 0)
        def _():
            total_ref[:, cut] = part

        @pl.when((step > 0) & (step < pl.num_programs(0) - 1))
        def _():
            total_ref[:, cut] = total_ref[:, cut] + part

        @pl.when(step == pl.num_programs(0) - 1)
        def _():
            out_ref[:, cut] = (total_ref[:, cut] + part).astype(BF16)


def expert(place, rows, weights, lines, columns, capacity):
    count, width = rows.shape
    half, units = weights[0].shape[1:]
    tile = 256
    weight = pl.BlockSpec((1, half, tile), lambda i: (0, 0, i))
    down = pl.BlockSpec((1, tile, half), lambda i: (0, i, 0))
    out = 2 * half + (META if lines else 0)
    return call(
        functools.partial(expert_kernel, lines=len(lines), capacity=capacity),
        "expert",
        pltpu.HBM((count, out), BF16),
        12 * count * half * units,
        2 * (count * width + 6 * half * units + count * out),
        44,
        grid=(units // tile,),
        in_specs=[SCALARS]
        + [weight] * 4
        + [down] * 2
        + [pl.BlockSpec((8, count), lambda i: (0, 0))] * len(lines)
        + [pl.BlockSpec((count, META), lambda i: (0, 0))] * len(columns)
        + [STAYS],
        out_specs=pl.BlockSpec((count, out), lambda i: (0, 0)),
        scratch_shapes=[
            pltpu.VMEM((count, 2 * half), F32),
            pltpu.VMEM((count, width), BF16),
            pltpu.SemaphoreType.DMA,
        ],
    )(place, *far_memory(*weights), *lines, *columns, *far_memory(rows))


def combine_kernel(table_ref, flag_ref, *refs, parts, pieces, groups, flag):
    part_refs, out_refs = refs[:parts], refs[parts : -parts - 2]
    kept_refs, built_ref, sent = refs[-parts - 2 : -2], refs[-2], refs[-1]
    tile = part_refs[0].shape[1]
    tok = out_refs[0].shape[0]
    blocks = len(out_refs) // pieces
    step, steps = pl.program_id(0), pl.num_programs(0)
    half = out_refs[-1].shape[1]

    @pl.when(step == 0)
    def _():
        table = table_ref[...].astype(F32) * lines_of(flag_ref[...], 8)[flag : flag + 1]
        total = jnp.sum(table, axis=1, keepdims=True)
        built_ref[:, 2 * half :] = jnp.broadcast_to(total, (blocks * tok, META)).astype(BF16)
        table = table.astype(BF16)
        columns = table.shape[1]
        first = 0
        for kept_ref in kept_refs:
            count = kept_ref.shape[1]
            part = count // groups
            if count == columns:
                kept_ref[...] = table
            else:
                source, lane = iota((columns, count), 0), iota((columns, count), 1)
                group = divided(lane, part, groups)
                taken = source == (columns // groups - part) * group + lane + first
                taken = taken.astype(F32).astype(BF16)
                kept_ref[...] = jnp.dot(table, taken, preferred_element_type=F32).astype(BF16)
            first += part

    total = None
    for kept_ref, part_ref in zip(kept_refs, part_refs):
        product = jnp.dot(kept_ref[...], part_ref[...], preferred_element_type=F32)
        total = product if total is None else total + product
    built_ref[:, pl.ds(pl.multiple_of(step * tile, 128), tile)] = total.astype(BF16)

    def copies(p):
        made = []
        for b in range(blocks):
            to = out_refs[p * blocks + b]
            source = built_ref.at[pl.ds(b * tok, tok), pl.ds((pieces - 1 - p) * half, to.shape[1])]
            made.append(pltpu.make_async_copy(source, to, sent.at[p, b]))
        return made

    for p in range(pieces):

        @pl.when(step == (pieces - p) * steps // pieces - 1)
        def _():
            for copy in copies(p):
                copy.start()

    @pl.when(step == steps - 1)
    def _():
        for p in range(pieces):
            for copy in copies(p):
                copy.wait()


def combine(table, far, parts, flag, half, blocks, groups):
    total, count = table.shape
    tok = total // blocks
    tile = half // 2
    last = far.shape[1] // META - 1
    return call(
        functools.partial(combine_kernel, parts=len(parts), pieces=2, groups=groups, flag=flag),
        "combine",
        (pltpu.HBM((tok, half + META), BF16),) * blocks + (pltpu.HBM((tok, half), BF16),) * blocks,
        4 * total * count * half,
        4 * (total * count + (count + total) * half),
        16,
        grid=(2 * half // tile,),
        in_specs=[
            pl.BlockSpec((total, count), lambda i: (0, 0)),
            pl.BlockSpec((count, META), lambda i: (0, last)),
        ]
        + [pl.BlockSpec((rows.shape[0], tile), lambda i: (0, i)) for rows in parts],
        out_specs=(STAYS,) * (2 * blocks),
        scratch_shapes=[pltpu.VMEM((total, rows.shape[0]), BF16) for rows in parts]
        + [
            pltpu.VMEM((total, 2 * half + META), BF16),
            pltpu.SemaphoreType.DMA((2, blocks)),
        ],
    )(*far_memory(table), far, *parts)


def per_device(
    activations, gate_weights, up_weights, down_weights, expert_ids, gate_scores, arrival_pos
):
    groups = lax.axis_size("group")
    members = lax.axis_size("ingroup")
    per_group = ring = members // 2
    tok = activations.shape[0]
    half = activations.shape[1] // 2
    top_picks = expert_ids.shape[1]
    capacity = 2 * top_picks * tok
    group_most = min(tok, 3 * tok * TOPG // (2 * groups))
    slots = (2 * group_most + per_group - 1) // per_group
    index = lax.axis_index("ingroup")
    place = jnp.stack([index // 2, index % 2]).astype(jnp.int32)
    partner = [(i, i ^ 1) for i in range(members)]

    def along(shard, by):
        hop = [(i, (i // 2 + by) % ring * 2 + i % 2) for i in range(members)]
        return lax.ppermute(shard, "ingroup", hop)

    def swap(shard):
        return lax.ppermute(shard, "ingroup", partner)

    def exchange(rows):
        return lax.all_to_all(rows, "group", split_axis=0, concat_axis=0, tiled=True)

    def gathered(shard, way):
        held = {0: shard}
        for step in range(1, ring // 2):
            held[-step] = along(held[1 - step], 1)
            held[step] = along(held[step - 1], -1)
        held[-ring // 2] = along(held[way * (ring // 2 - 1)], -way)
        return held

    def added(moving, part):
        return (moving.astype(F32) + part.astype(F32)).astype(BF16)

    def scattered(parts, way):
        sums = parts[0].astype(F32)
        for side in (way, -way):
            steps = [side * step for step in range(ring // 2 - 1, 0, -1)]
            moving = parts[-ring // 2] if side == way else parts[steps.pop(0)]
            for step in steps:
                moving = added(along(moving, side), parts[step])
            sums = sums + along(moving, side).astype(F32)
        return sums

    left, right = start_rows(activations, expert_ids, gate_scores, arrival_pos)
    lefts, rights = gathered(left, -1), gathered(right, 1)
    rows = slots * len(NEAR)
    blocks = len(NEAR)

    def picked(offsets):
        return pick_rows(
            place, [lefts[o] for o in offsets], [rights[o] for o in offsets],
            groups, per_group, slots, 0, 0, rows,
        )

    near_rows, near_meta = picked(NEAR)
    far_rows, far_meta = picked(FAR)
    far_rows, *own_weights = lax.optimization_barrier(
        (far_rows, gate_weights, up_weights, down_weights)
    )
    weights = [w for own in own_weights for w in (own, swap(own))]
    near_rows = exchange(near_rows)
    near_rows, far_rows = lax.optimization_barrier((near_rows, far_rows))
    far_rows = exchange(far_rows)
    near_line, near_column = slot_keys(place, [near_rows], groups, members, slots, NEAR)
    near_out = expert(place, near_rows, weights, [], [], capacity)
    far_rows, near_out, near_line = lax.optimization_barrier((far_rows, near_out, near_line))
    near_back = exchange(near_out)
    far_line, far_column = slot_keys(place, [far_rows], groups, members, slots, FAR)
    lines = [near_line, far_line]
    lines = lines + [swap(line) for line in lines]
    far_out = expert(place, far_rows, weights, lines, [near_column, far_column], capacity)
    near_back, far_out = lax.optimization_barrier((near_back, far_out))
    far_back = exchange(far_out)
    far_table = score_table(place, far_meta, groups, per_group, slots, blocks)
    near_table = score_table(place, near_meta, groups, per_group, slots, blocks)
    far_parts = combine(far_table, far_back, [far_back], 1, half, blocks, groups)
    near_parts = combine(near_table, far_back, [near_back], 0, half, blocks, groups)
    other, own = (
        scattered(
            dict(zip(FAR + NEAR, far_parts[i : i + blocks] + near_parts[i : i + blocks])), way
        )
        for i, way in ((0, 1), (blocks, -1))
    )
    weight_sum = jnp.maximum(other[:, half : half + 1], 1.0)
    own, other = own / weight_sum, other[:, :half] / weight_sum
    is_first = index % 2 == 0
    left = jnp.where(is_first, own, other)
    right = jnp.where(is_first, other, own)
    return jnp.concatenate([left, right], axis=1).astype(BF16)


def solution(mesh):
    rows = P(("group", "ingroup"), None)
    weights = P(("group", "ingroup"), None, None)
    return jax.shard_map(
        per_device,
        mesh=mesh,
        in_specs=(rows, weights, weights, weights, rows, rows, P(("group", "ingroup"))),
        out_specs=rows,
        check_vma=False,
    )
```

time: 289 us -> 273 us (0.945)
  local copies, waits for them, and re-layouts: 27.7 us -> 3.35 us
  waiting for transfers between devices: 146 us -> 123 us
  starting transfers between devices: 60 us -> 78.8 us
  Pallas kernels: 46.7 us -> 60.1 us
  other arithmetic: 5.72 us -> 2.75 us
    unnamed x72 -> x36, local copies, waits for them, and re-layouts: 26.3 us -> 3.35 us
    all_to_all x4, waiting for transfers between devices: 83.8 us -> 67 us  [exchange(): lax.all_to_all(rows, 'group', split_axis=0, concat_axis=0, tiled=True)]
    pallas_call x6 -> x7, Pallas kernels: 38.1 us -> 50.6 us  [the longest x2 38.9 us: expert(): call(functools.partial(expert_kernel, lines=len(lines), capacity=capacity...]
    ppermute x21 -> x28, waiting for transfers between devices: 61.5 us -> 50.2 us  [along(): return lax.ppermute(shard, 'ingroup', hop)]
    all_to_all x4, starting transfers between devices: 23.7 us -> 33.8 us  [exchange(): lax.all_to_all(rows, 'group', split_axis=0, concat_axis=0, tiled=True)]
    ppermute x21 -> x28, starting transfers between devices: 35.2 us -> 43.7 us  [along(): return lax.ppermute(shard, 'ingroup', hop)]
    ppermute x5, waiting for transfers between devices: 1.16 us -> 6.01 us  [swap(): return lax.ppermute(shard, 'ingroup', partner)]
  transfers between devices with their start and end apart: 30 -> 37, of which waited for: 17 -> 20; matrix products, arithmetic and copies ran while one was open for 1% -> 1% of each run, Pallas kernels for 15% -> 19%
where the time goes in v2:
time: 273 us; the launch traced here: 269 us
  waiting for transfers between devices  123 us (45%)
  starting transfers between devices  78.8 us (29%)
  Pallas kernels  60.1 us (22%)
  local copies, waits for them, and re-layouts  3.35 us (1%)
  other arithmetic  2.75 us (1%)
    all_to_all x4, waiting for transfers between devices, exchange(): lax.all_to_all(rows, 'group', split_axis=0, concat_axis=0, tiled=True)  67 us
    ppermute x28, waiting for transfers between devices, along(): return lax.ppermute(shard, 'ingroup', hop)  50.2 us
    ppermute x28, starting transfers between devices, along(): return lax.ppermute(shard, 'ingroup', hop)  43.7 us
    pallas_call x2, Pallas kernels, expert(): call(functools.partial(expert_kernel, lines=len(lines), capacity=capacity...  38.9 us
    all_to_all x4, starting transfers between devices, exchange(): lax.all_to_all(rows, 'group', split_axis=0, concat_axis=0, tiled=True)  33.8 us
    pallas_call x2, Pallas kernels, combine(): call(functools.partial(combine_kernel, parts=len(parts), pieces=2, groups...  8.48 us
    ppermute x5, waiting for transfers between devices, swap(): return lax.ppermute(shard, 'ingroup', partner)  6.01 us
    pallas_call x2, Pallas kernels, pick_rows(): call(functools.partial(pick_rows_kernel, groups=groups, per_group=per_gro...  5.63 us
  transfers between devices with their start and end apart: 37, of which 20 were waited for; matrix products, arithmetic and copies ran while one was open for 1% of the time, Pallas kernels for 19%

profile of v2, /device:TPU:8, one launch (start us, length us, event | category | flops | bytes accessed | tf_op | source)
XLA Modules:
  0.0 268.8 jit_solution(15316959851697672600)
XLA Ops:
  0.0 1.2 start_rows.1
  1.2 2.0 collective-permute-start.3
  3.2 1.9 collective-permute-start
  5.1 2.2 collective-permute-start.4
  7.3 6.6 %collective-permute-done.3.refs_5_ = bf16[64,1920]{1,0:T(8,128)(2,1)S(1)} collective-permute-done((bf16[64,1920]{1,0:T(8,128)(2,1)S(1)}, bf16[64,1920]{1,0:T(8,128)(2,1)S(1)}, u32[]{:S(2)}, u32[]{:S(2)}) %collective-permute-start.3) | collective-permute-done | bytes 245792 | tf_op jit(solution)/shard_map/ppermute | solution.py:452
  13.9 3.2 %collective-permute-start.1 = (bf16[64,1792]{1,0:T(8,128)(2,1)S(1)}, bf16[64,1792]{1,0:T(8,128)(2,1)S(1)}, u32[]{:S(2)}, u32[]{:S(2)}) collective-permute-start(bf16[64,1792]{1,0:T(8,128)(2,1)S(1)} %get-tuple-element.42.refs_0_), channel_id=1, source_target_pairs={{0,14},{1,15},{2,0},{3,1},{4,2},{5,3},{6,4},{7,5},{8,6},{9,7},{10,... | collective-permute-start | bytes 688136 | tf_op jit(solution)/shard_map/ppermute | solution.py:452
  17.2 1.7 collective-permute-done.refs_1_
  18.9 1.8 collective-permute-done.1.refs_2_
  20.7 7.5 %collective-permute-done.2.refs_3_ = bf16[64,1792]{1,0:T(8,128)(2,1)S(1)} collective-permute-done((bf16[64,1792]{1,0:T(8,128)(2,1)S(1)}, bf16[64,1792]{1,0:T(8,128)(2,1)S(1)}, u32[]{:S(2)}, u32[]{:S(2)}) %collective-permute-start.2) | collective-permute-done | bytes 229408 | tf_op jit(solution)/shard_map/ppermute | solution.py:452
  28.2 2.8 %pick_rows.2 = (bf16[384,3712]{1,0:T(8,128)(2,1)}, bf16[256,128]{1,0:T(8,128)(2,1)S(1)}) custom-call(s32[2]{0:T(128)S(1)} %pad_add_fusion.place_ref, bf16[64,1792]{1,0:T(8,128)(2,1)S(1)} %get-tuple-element.42.refs_0_, bf16[64,1792]{1,0:T(8,128)(2,1)S(1)} %collective-permute-done.refs_1_, bf16[64,1792]{1,0:T(8,128)(2,1)S(1)} %collective-permute-done.1.refs_2_, ...), custom_call_target="tpu_custom_call" | custom-call | flops 729808896 | bytes 4751360 | tf_op jit(solution)/shard_map/pick_rows/pallas_call | solution.py:140
  31.1 7.4 %all-to-all-start = ((bf16[16,24,3712]{2,1,0:T(8,128)(2,1)}), bf16[16,24,3712]{2,1,0:T(8,128)(2,1)S(1)}, u32[]{:S(2)}, u32[]{:S(2)}) async-start(bf16[16,24,3712]{2,1,0:T(8,128)(2,1)} %bitcast.19), calls=%async_computation | async-start | bytes 5701632 | tf_op jit(solution)/shard_map/all_to_all | solution.py:458
  38.5 1.7 collective-permute-start.10
  40.2 4.8 %collective-permute-done.10.refs_4_ = bf16[64,1920]{1,0:T(8,128)(2,1)S(1)} collective-permute-done((bf16[64,1920]{1,0:T(8,128)(2,1)S(1)}, bf16[64,1920]{1,0:T(8,128)(2,1)S(1)}, u32[]{:S(2)}, u32[]{:S(2)}) %collective-permute-start.10) | collective-permute-done | bytes 245792 | tf_op jit(solution)/shard_map/ppermute | solution.py:452
  45.0 2.6 collective-permute-start.12
  47.7 2.0 collective-permute-start.7
  49.7 4.2 %collective-permute-done.12.refs_6_ = bf16[64,1920]{1,0:T(8,128)(2,1)S(1)} collective-permute-done((bf16[64,1920]{1,0:T(8,128)(2,1)S(1)}, bf16[64,1920]{1,0:T(8,128)(2,1)S(1)}, u32[]{:S(2)}, u32[]{:S(2)}) %collective-permute-start.12) | collective-permute-done | bytes 245792 | tf_op jit(solution)/shard_map/ppermute | solution.py:452
  53.9 3.7 %collective-permute-start.13 = (bf16[64,1920]{1,0:T(8,128)(2,1)S(1)}, bf16[64,1920]{1,0:T(8,128)(2,1)S(1)}, u32[]{:S(2)}, u32[]{:S(2)}) collective-permute-start(bf16[64,1920]{1,0:T(8,128)(2,1)S(1)} %collective-permute-done.12.refs_6_), channel_id=1, source_target_pairs={{0,14},{1,15},{2,0},{3,1},{4,2},{5,3},{6,4},{7,5},{8,6},{9,7},{10,... | collective-permute-start | bytes 737288 | tf_op jit(solution)/shard_map/ppermute | solution.py:452
  57.6 1.3 collective-permute-done.6.refs_0_
  59.0 3.6 %collective-permute-start.8 = (bf16[64,1792]{1,0:T(8,128)(2,1)S(1)}, bf16[64,1792]{1,0:T(8,128)(2,1)S(1)}, u32[]{:S(2)}, u32[]{:S(2)}) collective-permute-start(bf16[64,1792]{1,0:T(8,128)(2,1)S(1)} %collective-permute-done.6.refs_0_), channel_id=1, source_target_pairs={{0,14},{1,15},{2,0},{3,1},{4,2},{5,3},{6,4},{7,5},{8,6},{9,7},{10,... | collective-permute-start | bytes 688136 | tf_op jit(solution)/shard_map/ppermute | solution.py:452
  62.8 3.3 %collective-permute-done.8.refs_2_ = bf16[64,1792]{1,0:T(8,128)(2,1)S(1)} collective-permute-done((bf16[64,1792]{1,0:T(8,128)(2,1)S(1)}, bf16[64,1792]{1,0:T(8,128)(2,1)S(1)}, u32[]{:S(2)}, u32[]{:S(2)}) %collective-permute-start.8) | collective-permute-done | bytes 229408 | tf_op jit(solution)/shard_map/ppermute | solution.py:452
  66.1 3.9 %collective-permute-done.9.refs_3_ = bf16[64,1792]{1,0:T(8,128)(2,1)S(1)} collective-permute-done((bf16[64,1792]{1,0:T(8,128)(2,1)S(1)}, bf16[64,1792]{1,0:T(8,128)(2,1)S(1)}, u32[]{:S(2)}, u32[]{:S(2)}) %collective-permute-start.9) | collective-permute-done | bytes 229408 | tf_op jit(solution)/shard_map/ppermute | solution.py:452
  70.0 2.8 %pick_rows.3 = (bf16[384,3712]{1,0:T(8,128)(2,1)}, bf16[256,128]{1,0:T(8,128)(2,1)S(1)}) custom-call(s32[2]{0:T(128)S(1)} %pad_add_fusion.place_ref, bf16[64,1792]{1,0:T(8,128)(2,1)S(1)} %collective-permute-done.6.refs_0_, bf16[64,1792]{1,0:T(8,128)(2,1)S(1)} %collective-permute-done.7.refs_1_, bf16[64,1792]{1,0:T(8,128)(2,1)S(1)} %collective-permute-done.8.refs_2_, ...), custom_call_target="tpu_custom_call" | custom-call | flops 729808896 | bytes 4751360 | tf_op jit(solution)/shard_map/pick_rows/pallas_call | solution.py:140
  73.5 4.6 %all-to-all-done = bf16[16,24,3712]{2,1,0:T(8,128)(2,1)S(1)} async-done(((bf16[16,24,3712]{2,1,0:T(8,128)(2,1)}), bf16[16,24,3712]{2,1,0:T(8,128)(2,1)S(1)}, u32[]{:S(2)}, u32[]{:S(2)}) %all-to-all-start) | async-done | bytes 2850848 | tf_op jit(solution)/shard_map/all_to_all | solution.py:458
  78.2 6.0 %all-to-all-start.1 = ((bf16[16,24,3712]{2,1,0:T(8,128)(2,1)}), bf16[16,24,3712]{2,1,0:T(8,128)(2,1)}, u32[]{:S(2)}, u32[]{:S(2)}) async-start(bf16[16,24,3712]{2,1,0:T(8,128)(2,1)} %bitcast.20), calls=%async_computation.1 | async-start | bytes 5701632 | tf_op jit(solution)/shard_map/all_to_all | solution.py:458
  85.0 5.2 %collective-permute-done.16.down_other = bf16[1,1024,1792]{2,1,0:T(8,128)(2,1)} collective-permute-done((bf16[1,1024,1792]{2,1,0:T(8,128)(2,1)}, bf16[1,1024,1792]{2,1,0:T(8,128)(2,1)}, u32[]{:S(2)}, u32[]{:S(2)}) %collective-permute-start.16) | collective-permute-done | bytes 3670048 | tf_op jit(solution)/shard_map/ppermute | solution.py:455
  90.2 19.4 %expert.2 = bf16[384,3584]{1,0:T(8,128)(2,1)} custom-call(s32[2]{0:T(128)S(1)} %pad_add_fusion.place_ref, bf16[1,1792,1024]{2,1,0:T(8,128)(2,1)} %gate_own.1, bf16[1,1792,1024]{2,1,0:T(8,128)(2,1)} %collective-permute-done.14.gate_other, bf16[1,1792,1024]{2,1,0:T(8,128)(2,1)} %up_own.1, bf16[1,1792,1024]{2,1,0:T(8,128)(2,1)} %collective-permute-done.15.up_other, ...), custom_call_target="tpu_custom_call" | custom-call | flops 8455716864 | bytes 27623424 | tf_op jit(solution)/shard_map/expert/pallas_call | solution.py:326
  109.6 11.3 %all-to-all-done.1 = bf16[16,24,3712]{2,1,0:T(8,128)(2,1)} async-done(((bf16[16,24,3712]{2,1,0:T(8,128)(2,1)}), bf16[16,24,3712]{2,1,0:T(8,128)(2,1)}, u32[]{:S(2)}, u32[]{:S(2)}) %all-to-all-start.1) | async-done | bytes 2850848 | tf_op jit(solution)/shard_map/all_to_all | solution.py:458
  120.9 5.3 %all-to-all-start.2 = ((bf16[16,24,3584]{2,1,0:T(8,128)(2,1)}), bf16[16,24,3584]{2,1,0:T(8,128)(2,1)S(1)}, u32[]{:S(2)}, u32[]{:S(2)}) async-start(bf16[16,24,3584]{2,1,0:T(8,128)(2,1)} %bitcast.22), calls=%async_computation.2 | async-start | bytes 5505024 | tf_op jit(solution)/shard_map/all_to_all | solution.py:458
  128.8 19.5 %expert.3 = bf16[384,3712]{1,0:T(8,128)(2,1)} custom-call(s32[2]{0:T(128)S(1)} %pad_add_fusion.place_ref, bf16[1,1792,1024]{2,1,0:T(8,128)(2,1)} %gate_own.1, bf16[1,1792,1024]{2,1,0:T(8,128)(2,1)} %collective-permute-done.14.gate_other, bf16[1,1792,1024]{2,1,0:T(8,128)(2,1)} %up_own.1, bf16[1,1792,1024]{2,1,0:T(8,128)(2,1)} %collective-permute-done.15.up_other, ...), custom_call_target="tpu_custom_call" | custom-call | flops 8455716864 | bytes 27721728 | tf_op jit(solution)/shard_map/expert/pallas_call | solution.py:326
  148.3 16.3 %all-to-all-done.2 = bf16[16,24,3584]{2,1,0:T(8,128)(2,1)S(1)} async-done(((bf16[16,24,3584]{2,1,0:T(8,128)(2,1)}), bf16[16,24,3584]{2,1,0:T(8,128)(2,1)S(1)}, u32[]{:S(2)}, u32[]{:S(2)}) %all-to-all-start.2) | async-done | bytes 2752544 | tf_op jit(solution)/shard_map/all_to_all | solution.py:458
  164.6 1.5 copy-done.1
  166.1 15.2 %all-to-all-start.3 = ((bf16[16,24,3712]{2,1,0:T(8,128)(2,1)}), bf16[16,24,3712]{2,1,0:T(8,128)(2,1)S(1)}, u32[]{:S(2)}, u32[]{:S(2)}) async-start(bf16[16,24,3712]{2,1,0:T(8,128)(2,1)} %bitcast.21), calls=%async_computation.3 | async-start | bytes 5701632 | tf_op jit(solution)/shard_map/all_to_all | solution.py:458
  181.3 1.9 score_table.3.table_ref
  183.3 34.7 %all-to-all-done.3 = bf16[16,24,3712]{2,1,0:T(8,128)(2,1)S(1)} async-done(((bf16[16,24,3712]{2,1,0:T(8,128)(2,1)}), bf16[16,24,3712]{2,1,0:T(8,128)(2,1)S(1)}, u32[]{:S(2)}, u32[]{:S(2)}) %all-to-all-start.3) | async-done | bytes 2850848 | tf_op jit(solution)/shard_map/all_to_all | solution.py:458
  217.9 4.2 %combine.3 = (bf16[64,1920]{1,0:T(8,128)(2,1)}, bf16[64,1920]{1,0:T(8,128)(2,1)}, bf16[64,1920]{1,0:T(8,128)(2,1)}, bf16[64,1920]{1,0:T(8,128)(2,1)}, bf16[64,17...) custom-call(bf16[256,384]{1,0:T(8,128)(2,1)} %score_table.3.table_ref, ...), custom_call_target="tpu_custom_call" | custom-call | flops 704643072 | bytes 4980736 | tf_op jit(solution)/shard_map/combine/pallas_call | solution.py:412
  222.2 1.2 collective-permute-start.19
  223.4 2.0 score_table.2.table_ref
  226.3 3.2 %collective-permute-start.30 = (bf16[64,1920]{1,0:T(8,128)(2,1)}, bf16[64,1920]{1,0:T(8,128)(2,1)S(1)}, u32[]{:S(2)}, u32[]{:S(2)}) collective-permute-start(bf16[64,1920]{1,0:T(8,128)(2,1)} %get-tuple-element.76), channel_id=1, source_target_pairs={{0,14},{1,15},{2,0},{3,1},{4,2},{5,3},{6,4},{7,5},{8,6},{9,7},{10,... | collective-permute-start | bytes 737288 | tf_op jit(solution)/shard_map/ppermute | solution.py:452
  229.5 1.8 copy-done.2
  231.3 4.2 %combine.2 = (bf16[64,1920]{1,0:T(8,128)(2,1)}, bf16[64,1920]{1,0:T(8,128)(2,1)}, bf16[64,1920]{1,0:T(8,128)(2,1)}, bf16[64,1920]{1,0:T(8,128)(2,1)}, bf16[64,17...) custom-call(bf16[256,384]{1,0:T(8,128)(2,1)} %score_table.2.table_ref, ...), custom_call_target="tpu_custom_call" | custom-call | flops 704643072 | bytes 4980736 | tf_op jit(solution)/shard_map/combine/pallas_call | solution.py:412
  239.1 3.3 %collective-permute-start.31 = (bf16[64,1920]{1,0:T(8,128)(2,1)S(1)}, bf16[64,1920]{1,0:T(8,128)(2,1)S(1)}, u32[]{:S(2)}, u32[]{:S(2)}) collective-permute-start(bf16[64,1920]{1,0:T(8,128)(2,1)S(1)} %add_convert_fusion.1), channel_id=1, source_target_pairs={{0,14},{1,15},{2,0},{3,1},{4,2},{5,3},{6,4},{7,5},{8,6},{9,7},{10,... | collective-permute-start | bytes 737288 | tf_op jit(solution)/shard_map/ppermute | solution.py:452
  242.4 1.6 collective-permute-done.20
  244.0 2.7 %collective-permute-start.21 = (bf16[64,1792]{1,0:T(8,128)(2,1)S(1)}, bf16[64,1792]{1,0:T(8,128)(2,1)S(1)}, u32[]{:S(2)}, u32[]{:S(2)}) collective-permute-start(bf16[64,1792]{1,0:T(8,128)(2,1)S(1)} %add_convert_fusion.8), channel_id=1, source_target_pairs={{0,14},{1,15},{2,0},{3,1},{4,2},{5,3},{6,4},{7,5},{8,6},{9,7},{10,... | collective-permute-start | bytes 688136 | tf_op jit(solution)/shard_map/ppermute | solution.py:452
  246.9 3.6 %collective-permute-done.27 = bf16[64,1920]{1,0:T(8,128)(2,1)S(1)} collective-permute-done((bf16[64,1920]{1,0:T(8,128)(2,1)S(1)}, bf16[64,1920]{1,0:T(8,128)(2,1)S(1)}, u32[]{:S(2)}, u32[]{:S(2)}) %collective-permute-start.27) | collective-permute-done | bytes 245792 | tf_op jit(solution)/shard_map/ppermute | solution.py:452
  251.1 2.9 %collective-permute-start.32 = (bf16[64,1920]{1,0:T(8,128)(2,1)S(1)}, bf16[64,1920]{1,0:T(8,128)(2,1)S(1)}, u32[]{:S(2)}, u32[]{:S(2)}) collective-permute-start(bf16[64,1920]{1,0:T(8,128)(2,1)S(1)} %add_convert_fusion), channel_id=1, source_target_pairs={{0,14},{1,15},{2,0},{3,1},{4,2},{5,3},{6,4},{7,5},{8,6},{9,7},{10,... | collective-permute-start | bytes 737288 | tf_op jit(solution)/shard_map/ppermute | solution.py:452
  254.0 5.8 %collective-permute-done.28 = bf16[64,1920]{1,0:T(8,128)(2,1)S(1)} collective-permute-done((bf16[64,1920]{1,0:T(8,128)(2,1)S(1)}, bf16[64,1920]{1,0:T(8,128)(2,1)S(1)}, u32[]{:S(2)}, u32[]{:S(2)}) %collective-permute-start.28) | collective-permute-done | bytes 245792 | tf_op jit(solution)/shard_map/ppermute | solution.py:452
  260.1 3.3 %collective-permute-start.22 = (bf16[64,1792]{1,0:T(8,128)(2,1)S(1)}, bf16[64,1792]{1,0:T(8,128)(2,1)S(1)}, u32[]{:S(2)}, u32[]{:S(2)}) collective-permute-start(bf16[64,1792]{1,0:T(8,128)(2,1)S(1)} %add_convert_fusion.7), channel_id=1, source_target_pairs={{0,14},{1,15},{2,0},{3,1},{4,2},{5,3},{6,4},{7,5},{8,6},{9,7},{10,... | collective-permute-start | bytes 688136 | tf_op jit(solution)/shard_map/ppermute | solution.py:452
  263.4 4.0 %collective-permute-done.29 = bf16[64,1920]{1,0:T(8,128)(2,1)S(1)} collective-permute-done((bf16[64,1920]{1,0:T(8,128)(2,1)S(1)}, bf16[64,1920]{1,0:T(8,128)(2,1)S(1)}, u32[]{:S(2)}, u32[]{:S(2)}) %collective-permute-start.29) | collective-permute-done | bytes 245792 | tf_op jit(solution)/shard_map/ppermute | solution.py:452
  (88 shorter events, 11.1 us)
Async XLA Ops:
  1.2 12.7 %collective-permute-start.3 = (bf16[64,1920]{1,0:T(8,128)(2,1)S(1)}, bf16[64,1920]{1,0:T(8,128)(2,1)S(1)}, u32[]{:S(2)}, u32[]{:S(2)}) collective-permute-start(bf16[64,1920]{1,0:T(8,128)(2,1)S(1)} %get-tuple-element.43.refs_4_), channel_id=1, source_target_pairs={{0,2},{1,3},{2,4},{3,5},{4,6},{5,7},{6,8},{7,9},{8,10},{9,11},{10,... | collective-permute-start | bytes 737288 | tf_op jit(solution)/shard_map/ppermute | solution.py:452
  3.2 15.6 %collective-permute-start = (bf16[64,1792]{1,0:T(8,128)(2,1)S(1)}, bf16[64,1792]{1,0:T(8,128)(2,1)S(1)}, u32[]{:S(2)}, u32[]{:S(2)}) collective-permute-start(bf16[64,1792]{1,0:T(8,128)(2,1)S(1)} %get-tuple-element.42.refs_0_), channel_id=1, source_target_pairs={{0,2},{1,3},{2,4},{3,5},{4,6},{5,7},{6,8},{7,9},{8,10},{9,11},{10,... | collective-permute-start | bytes 688136 | tf_op jit(solution)/shard_map/ppermute | solution.py:452
  5.1 15.6 %collective-permute-start.4 = (bf16[64,1920]{1,0:T(8,128)(2,1)S(1)}, bf16[64,1920]{1,0:T(8,128)(2,1)S(1)}, u32[]{:S(2)}, u32[]{:S(2)}) collective-permute-start(bf16[64,1920]{1,0:T(8,128)(2,1)S(1)} %get-tuple-element.43.refs_4_), channel_id=1, source_target_pairs={{0,14},{1,15},{2,0},{3,1},{4,2},{5,3},{6,4},{7,5},{8,6},{9,7},{10,... | collective-permute-start | bytes 737288 | tf_op jit(solution)/shard_map/ppermute | solution.py:452
  13.9 14.3 %collective-permute-start.5 = (bf16[64,1920]{1,0:T(8,128)(2,1)S(1)}, bf16[64,1920]{1,0:T(8,128)(2,1)S(1)}, u32[]{:S(2)}, u32[]{:S(2)}) collective-permute-start(bf16[64,1920]{1,0:T(8,128)(2,1)S(1)} %collective-permute-done.3.refs_5_), channel_id=1, source_target_pairs={{0,2},{1,3},{2,4},{3,5},{4,6},{5,7},{6,8},{7,9},{8,10},{9,11},{10,... | collective-permute-start | bytes 737288 | tf_op jit(solution)/shard_map/ppermute | solution.py:452
  13.9 6.8 %collective-permute-start.1 = (bf16[64,1792]{1,0:T(8,128)(2,1)S(1)}, bf16[64,1792]{1,0:T(8,128)(2,1)S(1)}, u32[]{:S(2)}, u32[]{:S(2)}) collective-permute-start(bf16[64,1792]{1,0:T(8,128)(2,1)S(1)} %get-tuple-element.42.refs_0_), channel_id=1, source_target_pairs={{0,14},{1,15},{2,0},{3,1},{4,2},{5,3},{6,4},{7,5},{8,6},{9,7},{10,... | collective-permute-start | bytes 688136 | tf_op jit(solution)/shard_map/ppermute | solution.py:452
  18.8 9.4 %collective-permute-start.2 = (bf16[64,1792]{1,0:T(8,128)(2,1)S(1)}, bf16[64,1792]{1,0:T(8,128)(2,1)S(1)}, u32[]{:S(2)}, u32[]{:S(2)}) collective-permute-start(bf16[64,1792]{1,0:T(8,128)(2,1)S(1)} %collective-permute-done.refs_1_), channel_id=1, source_target_pairs={{0,2},{1,3},{2,4},{3,5},{4,6},{5,7},{6,8},{7,9},{8,10},{9,11},{10,... | collective-permute-start | bytes 688136 | tf_op jit(solution)/shard_map/ppermute | solution.py:452
  20.7 10.3 %copy-start.4 = (bf16[64,1792]{1,0:T(8,128)(2,1)}, bf16[64,1792]{1,0:T(8,128)(2,1)S(1)}, u32[]{:S(2)}) copy-start(bf16[64,1792]{1,0:T(8,128)(2,1)S(1)} %collective-permute-done.1.refs_2_) | copy-start | bytes 688132
  31.1 47.1 %all-to-all-start = ((bf16[16,24,3712]{2,1,0:T(8,128)(2,1)}), bf16[16,24,3712]{2,1,0:T(8,128)(2,1)S(1)}, u32[]{:S(2)}, u32[]{:S(2)}) async-start(bf16[16,24,3712]{2,1,0:T(8,128)(2,1)} %bitcast.19), calls=%async_computation | async-start | bytes 5701632 | tf_op jit(solution)/shard_map/all_to_all | solution.py:458
  38.5 6.6 %collective-permute-start.10 = (bf16[64,1920]{1,0:T(8,128)(2,1)S(1)}, bf16[64,1920]{1,0:T(8,128)(2,1)S(1)}, u32[]{:S(2)}, u32[]{:S(2)}) collective-permute-start(bf16[64,1920]{1,0:T(8,128)(2,1)S(1)} %collective-permute-done.4.refs_6_), channel_id=1, source_target_pairs={{0,14},{1,15},{2,0},{3,1},{4,2},{5,3},{6,4},{7,5},{8,6},{9,7},{10,... | collective-permute-start | bytes 737288 | tf_op jit(solution)/shard_map/ppermute | solution.py:452
  45.0 8.9 %collective-permute-start.12 = (bf16[64,1920]{1,0:T(8,128)(2,1)S(1)}, bf16[64,1920]{1,0:T(8,128)(2,1)S(1)}, u32[]{:S(2)}, u32[]{:S(2)}) collective-permute-start(bf16[64,1920]{1,0:T(8,128)(2,1)S(1)} %collective-permute-done.10.refs_4_), channel_id=1, source_target_pairs={{0,14},{1,15},{2,0},{3,1},{4,2},{5,3},{6,4},{7,5},{8,6},{9,7},{10,... | collective-permute-start | bytes 737288 | tf_op jit(solution)/shard_map/ppermute | solution.py:452
  47.7 11.3 %collective-permute-start.6 = (bf16[64,1792]{1,0:T(8,128)(2,1)}, bf16[64,1792]{1,0:T(8,128)(2,1)S(1)}, u32[]{:S(2)}, u32[]{:S(2)}) collective-permute-start(bf16[64,1792]{1,0:T(8,128)(2,1)} %copy-done.4), channel_id=1, source_target_pairs={{0,14},{1,15},{2,0},{3,1},{4,2},{5,3},{6,4},{7,5},{8,6},{9,7},{10,... | collective-permute-start | bytes 688136 | tf_op jit(solution)/shard_map/ppermute | solution.py:452
  47.7 14.8 %collective-permute-start.7 = (bf16[64,1792]{1,0:T(8,128)(2,1)}, bf16[64,1792]{1,0:T(8,128)(2,1)S(1)}, u32[]{:S(2)}, u32[]{:S(2)}) collective-permute-start(bf16[64,1792]{1,0:T(8,128)(2,1)} %copy-done.3), channel_id=1, source_target_pairs={{0,2},{1,3},{2,4},{3,5},{4,6},{5,7},{6,8},{7,9},{8,10},{9,11},{10,... | collective-permute-start | bytes 688136 | tf_op jit(solution)/shard_map/ppermute | solution.py:452
  49.7 16.4 %collective-permute-start.11 = (bf16[64,1920]{1,0:T(8,128)(2,1)S(1)}, bf16[64,1920]{1,0:T(8,128)(2,1)S(1)}, u32[]{:S(2)}, u32[]{:S(2)}) collective-permute-start(bf16[64,1920]{1,0:T(8,128)(2,1)S(1)} %collective-permute-done.5.refs_7_), channel_id=1, source_target_pairs={{0,2},{1,3},{2,4},{3,5},{4,6},{5,7},{6,8},{7,9},{8,10},{9,11},{10,... | collective-permute-start | bytes 737288 | tf_op jit(solution)/shard_map/ppermute | solution.py:452
  53.9 16.1 %collective-permute-start.13 = (bf16[64,1920]{1,0:T(8,128)(2,1)S(1)}, bf16[64,1920]{1,0:T(8,128)(2,1)S(1)}, u32[]{:S(2)}, u32[]{:S(2)}) collective-permute-start(bf16[64,1920]{1,0:T(8,128)(2,1)S(1)} %collective-permute-done.12.refs_6_), channel_id=1, source_target_pairs={{0,14},{1,15},{2,0},{3,1},{4,2},{5,3},{6,4},{7,5},{8,6},{9,7},{10,... | collective-permute-start | bytes 737288 | tf_op jit(solution)/shard_map/ppermute | solution.py:452
  59.0 7.1 %collective-permute-start.8 = (bf16[64,1792]{1,0:T(8,128)(2,1)S(1)}, bf16[64,1792]{1,0:T(8,128)(2,1)S(1)}, u32[]{:S(2)}, u32[]{:S(2)}) collective-permute-start(bf16[64,1792]{1,0:T(8,128)(2,1)S(1)} %collective-permute-done.6.refs_0_), channel_id=1, source_target_pairs={{0,14},{1,15},{2,0},{3,1},{4,2},{5,3},{6,4},{7,5},{8,6},{9,7},{10,... | collective-permute-start | bytes 688136 | tf_op jit(solution)/shard_map/ppermute | solution.py:452
  62.5 7.5 %collective-permute-start.9 = (bf16[64,1792]{1,0:T(8,128)(2,1)S(1)}, bf16[64,1792]{1,0:T(8,128)(2,1)S(1)}, u32[]{:S(2)}, u32[]{:S(2)}) collective-permute-start(bf16[64,1792]{1,0:T(8,128)(2,1)S(1)} %collective-permute-done.7.refs_1_), channel_id=1, source_target_pairs={{0,2},{1,3},{2,4},{3,5},{4,6},{5,7},{6,8},{7,9},{8,10},{9,11},{10,... | collective-permute-start | bytes 688136 | tf_op jit(solution)/shard_map/ppermute | solution.py:452
  72.8 12.1 %collective-permute-start.14 = (bf16[1,1792,1024]{2,1,0:T(8,128)(2,1)}, bf16[1,1792,1024]{2,1,0:T(8,128)(2,1)}, u32[]{:S(2)}, u32[]{:S(2)}) collective-permute-start(bf16[1,1792,1024]{2,1,0:T(8,128)(2,1)} %gate_own.1), channel_id=1, source_target_pairs={{0,1},{1,0},{2,3},{3,2},{4,5},{5,4},{6,7},{7,6},{8,9},{9,8},{10,11... | collective-permute-start | bytes 11010056 | tf_op jit(solution)/shard_map/ppermute | solution.py:455
  72.9 12.1 %collective-permute-start.15 = (bf16[1,1792,1024]{2,1,0:T(8,128)(2,1)}, bf16[1,1792,1024]{2,1,0:T(8,128)(2,1)}, u32[]{:S(2)}, u32[]{:S(2)}) collective-permute-start(bf16[1,1792,1024]{2,1,0:T(8,128)(2,1)} %up_own.1), channel_id=1, source_target_pairs={{0,1},{1,0},{2,3},{3,2},{4,5},{5,4},{6,7},{7,6},{8,9},{9,8},{10,11... | collective-permute-start | bytes 11010056 | tf_op jit(solution)/shard_map/ppermute | solution.py:455
  73.4 16.7 %collective-permute-start.16 = (bf16[1,1024,1792]{2,1,0:T(8,128)(2,1)}, bf16[1,1024,1792]{2,1,0:T(8,128)(2,1)}, u32[]{:S(2)}, u32[]{:S(2)}) collective-permute-start(bf16[1,1024,1792]{2,1,0:T(8,128)(2,1)} %down_own.1), channel_id=1, source_target_pairs={{0,1},{1,0},{2,3},{3,2},{4,5},{5,4},{6,7},{7,6},{8,9},{9,8},{10,11... | collective-permute-start | bytes 11010056 | tf_op jit(solution)/shard_map/ppermute | solution.py:455
  78.2 42.7 %all-to-all-start.1 = ((bf16[16,24,3712]{2,1,0:T(8,128)(2,1)}), bf16[16,24,3712]{2,1,0:T(8,128)(2,1)}, u32[]{:S(2)}, u32[]{:S(2)}) async-start(bf16[16,24,3712]{2,1,0:T(8,128)(2,1)} %bitcast.20), calls=%async_computation.1 | async-start | bytes 5701632 | tf_op jit(solution)/shard_map/all_to_all | solution.py:458
  85.0 24.6 %copy-start.5 = (f32[384,128]{1,0:T(8,128)}, f32[384,128]{1,0:T(8,128)S(1)}, u32[]{:S(2)}) copy-start(f32[384,128]{1,0:T(8,128)S(1)} %get-tuple-element.58.refs_4_) | copy-start | bytes 589828
  120.9 7.9 %copy-start.6 = (f32[384,128]{1,0:T(8,128)S(1)}, f32[384,128]{1,0:T(8,128)}, u32[]{:S(2)}) copy-start(f32[384,128]{1,0:T(8,128)} %copy-done.5) | copy-start | bytes 589828
  120.9 43.7 %all-to-all-start.2 = ((bf16[16,24,3584]{2,1,0:T(8,128)(2,1)}), bf16[16,24,3584]{2,1,0:T(8,128)(2,1)S(1)}, u32[]{:S(2)}, u32[]{:S(2)}) async-start(bf16[16,24,3584]{2,1,0:T(8,128)(2,1)} %bitcast.22), calls=%async_computation.2 | async-start | bytes 5505024 | tf_op jit(solution)/shard_map/all_to_all | solution.py:458
  127.4 1.3 collective-permute-start.18
  127.5 1.3 collective-permute-start.17
  166.1 51.8 %all-to-all-start.3 = ((bf16[16,24,3712]{2,1,0:T(8,128)(2,1)}), bf16[16,24,3712]{2,1,0:T(8,128)(2,1)S(1)}, u32[]{:S(2)}, u32[]{:S(2)}) async-start(bf16[16,24,3712]{2,1,0:T(8,128)(2,1)} %bitcast.21), calls=%async_computation.3 | async-start | bytes 5701632 | tf_op jit(solution)/shard_map/all_to_all | solution.py:458
  222.2 13.4 %collective-permute-start.19 = (bf16[64,1792]{1,0:T(8,128)(2,1)}, bf16[64,1792]{1,0:T(8,128)(2,1)S(1)}, u32[]{:S(2)}, u32[]{:S(2)}) collective-permute-start(bf16[64,1792]{1,0:T(8,128)(2,1)} %get-tuple-element.64), channel_id=1, source_target_pairs={{0,14},{1,15},{2,0},{3,1},{4,2},{5,3},{6,4},{7,5},{8,6},{9,7},{10,... | collective-permute-start | bytes 688136 | tf_op jit(solution)/shard_map/ppermute | solution.py:452
  225.3 11.5 %collective-permute-start.23 = (bf16[64,1792]{1,0:T(8,128)(2,1)}, bf16[64,1792]{1,0:T(8,128)(2,1)S(1)}, u32[]{:S(2)}, u32[]{:S(2)}) collective-permute-start(bf16[64,1792]{1,0:T(8,128)(2,1)} %get-tuple-element.68), channel_id=1, source_target_pairs={{0,2},{1,3},{2,4},{3,5},{4,6},{5,7},{6,8},{7,9},{8,10},{9,11},{10,... | collective-permute-start | bytes 688136 | tf_op jit(solution)/shard_map/ppermute | solution.py:452
  226.2 11.7 %collective-permute-start.26 = (bf16[64,1920]{1,0:T(8,128)(2,1)}, bf16[64,1920]{1,0:T(8,128)(2,1)S(1)}, u32[]{:S(2)}, u32[]{:S(2)}) collective-permute-start(bf16[64,1920]{1,0:T(8,128)(2,1)} %get-tuple-element.72), channel_id=1, source_target_pairs={{0,2},{1,3},{2,4},{3,5},{4,6},{5,7},{6,8},{7,9},{8,10},{9,11},{10,... | collective-permute-start | bytes 737288 | tf_op jit(solution)/shard_map/ppermute | solution.py:452
  226.3 11.8 %collective-permute-start.30 = (bf16[64,1920]{1,0:T(8,128)(2,1)}, bf16[64,1920]{1,0:T(8,128)(2,1)S(1)}, u32[]{:S(2)}, u32[]{:S(2)}) collective-permute-start(bf16[64,1920]{1,0:T(8,128)(2,1)} %get-tuple-element.76), channel_id=1, source_target_pairs={{0,14},{1,15},{2,0},{3,1},{4,2},{5,3},{6,4},{7,5},{8,6},{9,7},{10,... | collective-permute-start | bytes 737288 | tf_op jit(solution)/shard_map/ppermute | solution.py:452
  235.5 8.5 %copy-start.15 = (bf16[64,1792]{1,0:T(8,128)(2,1)S(1)}, bf16[64,1792]{1,0:T(8,128)(2,1)}, u32[]{:S(2)}) copy-start(bf16[64,1792]{1,0:T(8,128)(2,1)} %get-tuple-element.66) | copy-start | bytes 688132
  235.5 11.2 %copy-start.14 = (bf16[64,1792]{1,0:T(8,128)(2,1)S(1)}, bf16[64,1792]{1,0:T(8,128)(2,1)}, u32[]{:S(2)}) copy-start(bf16[64,1792]{1,0:T(8,128)(2,1)} %get-tuple-element.70) | copy-start | bytes 688132
  235.5 15.0 %copy-start.8 = (bf16[64,1920]{1,0:T(8,128)(2,1)S(1)}, bf16[64,1920]{1,0:T(8,128)(2,1)}, u32[]{:S(2)}) copy-start(bf16[64,1920]{1,0:T(8,128)(2,1)} %get-tuple-element.74) | copy-start | bytes 737284
  235.5 15.5 %copy-start.10 = (bf16[64,1920]{1,0:T(8,128)(2,1)S(1)}, bf16[64,1920]{1,0:T(8,128)(2,1)}, u32[]{:S(2)}) copy-start(bf16[64,1920]{1,0:T(8,128)(2,1)} %get-tuple-element.78) | copy-start | bytes 737284
  235.6 24.3 %copy-start.9 = (bf16[64,1920]{1,0:T(8,128)(2,1)S(1)}, bf16[64,1920]{1,0:T(8,128)(2,1)}, u32[]{:S(2)}) copy-start(bf16[64,1920]{1,0:T(8,128)(2,1)} %get-tuple-element.75) | copy-start | bytes 737284
  235.6 8.3 %collective-permute-start.20 = (bf16[64,1792]{1,0:T(8,128)(2,1)S(1)}, bf16[64,1792]{1,0:T(8,128)(2,1)S(1)}, u32[]{:S(2)}, u32[]{:S(2)}) collective-permute-start(bf16[64,1792]{1,0:T(8,128)(2,1)S(1)} %add_convert_fusion.9), channel_id=1, source_target_pairs={{0,14},{1,15},{2,0},{3,1},{4,2},{5,3},{6,4},{7,5},{8,6},{9,7},{10,... | collective-permute-start | bytes 688136 | tf_op jit(solution)/shard_map/ppermute | solution.py:452
  236.9 23.2 %copy-start.13 = (bf16[64,1792]{1,0:T(8,128)(2,1)S(1)}, bf16[64,1792]{1,0:T(8,128)(2,1)}, u32[]{:S(2)}) copy-start(bf16[64,1792]{1,0:T(8,128)(2,1)} %get-tuple-element.67) | copy-start | bytes 688132
  236.9 9.8 %collective-permute-start.24 = (bf16[64,1792]{1,0:T(8,128)(2,1)S(1)}, bf16[64,1792]{1,0:T(8,128)(2,1)S(1)}, u32[]{:S(2)}, u32[]{:S(2)}) collective-permute-start(bf16[64,1792]{1,0:T(8,128)(2,1)S(1)} %add_convert_fusion.6), channel_id=1, source_target_pairs={{0,2},{1,3},{2,4},{3,5},{4,6},{5,7},{6,8},{7,9},{8,10},{9,11},{10,... | collective-permute-start | bytes 688136 | tf_op jit(solution)/shard_map/ppermute | solution.py:452
  237.9 29.5 %copy-start.7 = (bf16[64,1920]{1,0:T(8,128)(2,1)S(1)}, bf16[64,1920]{1,0:T(8,128)(2,1)}, u32[]{:S(2)}) copy-start(bf16[64,1920]{1,0:T(8,128)(2,1)} %get-tuple-element.71) | copy-start | bytes 737284
  238.0 12.5 %collective-permute-start.27 = (bf16[64,1920]{1,0:T(8,128)(2,1)S(1)}, bf16[64,1920]{1,0:T(8,128)(2,1)S(1)}, u32[]{:S(2)}, u32[]{:S(2)}) collective-permute-start(bf16[64,1920]{1,0:T(8,128)(2,1)S(1)} %add_convert_fusion.4), channel_id=1, source_target_pairs={{0,2},{1,3},{2,4},{3,5},{4,6},{5,7},{6,8},{7,9},{8,10},{9,11},{10,... | collective-permute-start | bytes 737288 | tf_op jit(solution)/shard_map/ppermute | solution.py:452
  239.1 28.5 %copy-start.12 = (bf16[64,1792]{1,0:T(8,128)(2,1)S(1)}, bf16[64,1792]{1,0:T(8,128)(2,1)}, u32[]{:S(2)}) copy-start(bf16[64,1792]{1,0:T(8,128)(2,1)} %get-tuple-element.62) | copy-start | bytes 688132
  239.1 11.9 %collective-permute-start.31 = (bf16[64,1920]{1,0:T(8,128)(2,1)S(1)}, bf16[64,1920]{1,0:T(8,128)(2,1)S(1)}, u32[]{:S(2)}, u32[]{:S(2)}) collective-permute-start(bf16[64,1920]{1,0:T(8,128)(2,1)S(1)} %add_convert_fusion.1), channel_id=1, source_target_pairs={{0,14},{1,15},{2,0},{3,1},{4,2},{5,3},{6,4},{7,5},{8,6},{9,7},{10,... | collective-permute-start | bytes 737288 | tf_op jit(solution)/shard_map/ppermute | solution.py:452
  244.0 16.0 %collective-permute-start.21 = (bf16[64,1792]{1,0:T(8,128)(2,1)S(1)}, bf16[64,1792]{1,0:T(8,128)(2,1)S(1)}, u32[]{:S(2)}, u32[]{:S(2)}) collective-permute-start(bf16[64,1792]{1,0:T(8,128)(2,1)S(1)} %add_convert_fusion.8), channel_id=1, source_target_pairs={{0,14},{1,15},{2,0},{3,1},{4,2},{5,3},{6,4},{7,5},{8,6},{9,7},{10,... | collective-permute-start | bytes 688136 | tf_op jit(solution)/shard_map/ppermute | solution.py:452
  246.8 20.8 %collective-permute-start.25 = (bf16[64,1792]{1,0:T(8,128)(2,1)S(1)}, bf16[64,1792]{1,0:T(8,128)(2,1)S(1)}, u32[]{:S(2)}, u32[]{:S(2)}) collective-permute-start(bf16[64,1792]{1,0:T(8,128)(2,1)S(1)} %add_convert_fusion.5), channel_id=1, source_target_pairs={{0,2},{1,3},{2,4},{3,5},{4,6},{5,7},{6,8},{7,9},{8,10},{9,11},{10,... | collective-permute-start | bytes 688136 | tf_op jit(solution)/shard_map/ppermute | solution.py:452
  250.6 9.3 %collective-permute-start.28 = (bf16[64,1920]{1,0:T(8,128)(2,1)S(1)}, bf16[64,1920]{1,0:T(8,128)(2,1)S(1)}, u32[]{:S(2)}, u32[]{:S(2)}) collective-permute-start(bf16[64,1920]{1,0:T(8,128)(2,1)S(1)} %add_convert_fusion.3), channel_id=1, source_target_pairs={{0,2},{1,3},{2,4},{3,5},{4,6},{5,7},{6,8},{7,9},{8,10},{9,11},{10,... | collective-permute-start | bytes 737288 | tf_op jit(solution)/shard_map/ppermute | solution.py:452
  251.1 12.3 %collective-permute-start.32 = (bf16[64,1920]{1,0:T(8,128)(2,1)S(1)}, bf16[64,1920]{1,0:T(8,128)(2,1)S(1)}, u32[]{:S(2)}, u32[]{:S(2)}) collective-permute-start(bf16[64,1920]{1,0:T(8,128)(2,1)S(1)} %add_convert_fusion), channel_id=1, source_target_pairs={{0,14},{1,15},{2,0},{3,1},{4,2},{5,3},{6,4},{7,5},{8,6},{9,7},{10,... | collective-permute-start | bytes 737288 | tf_op jit(solution)/shard_map/ppermute | solution.py:452
  259.9 7.5 %collective-permute-start.29 = (bf16[64,1920]{1,0:T(8,128)(2,1)S(1)}, bf16[64,1920]{1,0:T(8,128)(2,1)S(1)}, u32[]{:S(2)}, u32[]{:S(2)}) collective-permute-start(bf16[64,1920]{1,0:T(8,128)(2,1)S(1)} %add_convert_fusion.2), channel_id=1, source_target_pairs={{0,2},{1,3},{2,4},{3,5},{4,6},{5,7},{6,8},{7,9},{8,10},{9,11},{10,... | collective-permute-start | bytes 737288 | tf_op jit(solution)/shard_map/ppermute | solution.py:452
  260.1 7.5 %collective-permute-start.22 = (bf16[64,1792]{1,0:T(8,128)(2,1)S(1)}, bf16[64,1792]{1,0:T(8,128)(2,1)S(1)}, u32[]{:S(2)}, u32[]{:S(2)}) collective-permute-start(bf16[64,1792]{1,0:T(8,128)(2,1)S(1)} %add_convert_fusion.7), channel_id=1, source_target_pairs={{0,14},{1,15},{2,0},{3,1},{4,2},{5,3},{6,4},{7,5},{8,6},{9,7},{10,... | collective-permute-start | bytes 688136 | tf_op jit(solution)/shard_map/ppermute | solution.py:452
  (7 other events, 28.6 us)
